TPU v7x, 512 devices: a whole 4x8x8 slice. The times are simulated.
512 devices in a mesh: var: 16 (over y, core), seq: 32 (over x, z).
Axes of the slice: x: 4, y: 8, z: 8, core: 2. Of those that a mesh axis runs over, the one named last changes fastest.
Arguments:
- tokens: bfloat16 [48, 2048, 4096], P('var', 'seq'), may hold values from -6 to 6
- agg_query: bfloat16 [32, 4096], replicated, may hold values from -2.109375 to 2.109375
- agg_value: bfloat16 [4096, 4096], P('var', 'seq'), may hold values from -0.09375 to 0.09375
- w_query: bfloat16 [4096, 4096], P('var', 'seq'), may hold values from -0.09375 to 0.09375
- w_key: bfloat16 [4096, 4096], P('var', 'seq'), may hold values from -0.09375 to 0.09375
- w_value: bfloat16 [4096, 4096], P('var', 'seq'), may hold values from -0.09375 to 0.09375
- gain: float32 [4096], replicated, may hold values from 0.25 to 1.75
- d_out: bfloat16 [32, 64, 4096], P(None, 'var', 'seq'), may hold values from -6 to 6
Outputs:
- attended: bfloat16 [32, 64, 4096], P(None, 'var', 'seq')
- d_tokens: bfloat16 [48, 2048, 4096], P('var', 'seq')
- d_query: float32 [32, 4096], replicated
All inputs are finite; a program needn't handle non-finite values.
Results may differ from a plain program's by a relative error of at most 0.035.
Values may be sent and summed in bfloat16 or wider, within the bound.
A program may use at most 64 MiB of HBM per device.

v0:
```python
import jax
import jax.numpy as jnp
from jax import lax
from jax.sharding import PartitionSpec as P

HD = 128


EPS = 1e-05


def per_device(tokens, agg_query, agg_value, w_query, w_key, w_value, gain, d_out):
    factor = HD ** (-0.5)
    grouped = lax.all_to_all(tokens, "var", split_axis=1, concat_axis=0, tiled=True)
    scores = (
        jnp.einsum("vrd,hd->vrh", grouped, agg_query, preferred_element_type=jnp.float32) * factor
    )
    mixw = jax.nn.softmax(scores, axis=0)
    mix_b = mixw.astype(jnp.bfloat16)
    summary = jnp.einsum("vrh,vrd->rhd", mix_b, grouped, preferred_element_type=jnp.float32).astype(
        jnp.bfloat16
    )
    heads_here = lax.all_to_all(summary, "seq", split_axis=1, concat_axis=0, tiled=True)
    row_count, head_count, width = heads_here.shape
    col_count = head_count * HD
    value_cols = lax.all_gather(agg_value, "var", axis=0, tiled=True)
    value_heads = value_cols.reshape(width, head_count, HD)
    pooled = jnp.einsum("rhd,dhe->rhe", heads_here, value_heads, preferred_element_type=jnp.float32)
    pooled = pooled.reshape(row_count, col_count).astype(jnp.bfloat16)
    first_col = lax.axis_index("seq") * col_count
    full_rows = lax.all_gather(pooled, "seq", axis=1, tiled=True).astype(jnp.float32)
    center = jnp.mean(full_rows, axis=1, keepdims=True)
    spread = jnp.mean((full_rows - center) ** 2, axis=1, keepdims=True)
    inv_std = lax.rsqrt(spread + EPS)
    unit_full = (full_rows - center) * inv_std
    normed = (unit_full * gain).astype(jnp.bfloat16)
    unit_share = lax.dynamic_slice_in_dim(unit_full, first_col, col_count, 1)
    wq_cols, wk_cols, wv_cols = (
        lax.all_gather(w_query, "var", axis=0, tiled=True),
        lax.all_gather(w_key, "var", axis=0, tiled=True),
        lax.all_gather(w_value, "var", axis=0, tiled=True),
    )
    queries = jnp.dot(normed, wq_cols, preferred_element_type=jnp.float32).astype(jnp.bfloat16)
    keys_here = jnp.dot(normed, wk_cols, preferred_element_type=jnp.float32).astype(jnp.bfloat16)
    values_here = jnp.dot(normed, wv_cols, preferred_element_type=jnp.float32).astype(jnp.bfloat16)
    all_keys, all_values = (
        lax.all_gather(keys_here, "var", axis=0, tiled=True),
        lax.all_gather(values_here, "var", axis=0, tiled=True),
    )
    grad_out = d_out.reshape(row_count, col_count)
    outputs, dqueries, dkeys, dvals = ([], [], [], [])
    logits = jnp.einsum("qe,ke->qk", queries, all_keys, preferred_element_type=jnp.float32) * factor
    top = jnp.max(logits, axis=1, keepdims=True)
    expo = jnp.exp(logits - top)
    total = jnp.sum(expo, axis=1, keepdims=True)
    probs = expo / total
    probs_b = probs.astype(jnp.bfloat16)
    outputs.append(
        jnp.dot(probs_b, all_values, preferred_element_type=jnp.float32).astype(jnp.bfloat16)
    )
    dprob = jnp.einsum("qe,ke->qk", grad_out, all_values, preferred_element_type=jnp.float32)
    inner = jnp.sum(probs * dprob, axis=1, keepdims=True)
    dlogit = (probs * (dprob - inner) * factor).astype(jnp.bfloat16)
    dqueries.append(
        jnp.dot(dlogit, all_keys, preferred_element_type=jnp.float32).astype(jnp.bfloat16)
    )
    dkeys.append(jnp.einsum("qk,qe->ke", dlogit, queries, preferred_element_type=jnp.float32))
    dvals.append(jnp.einsum("qk,qe->ke", probs_b, grad_out, preferred_element_type=jnp.float32))
    attended = outputs[0].reshape(d_out.shape)
    dquery = dqueries[0]
    dkey_sum, dval_sum = (
        lax.psum_scatter(
            dkeys[0].astype(jnp.bfloat16), "var", scatter_dimension=0, tiled=True
        ).astype(jnp.float32),
        lax.psum_scatter(
            dvals[0].astype(jnp.bfloat16), "var", scatter_dimension=0, tiled=True
        ).astype(jnp.float32),
    )
    dkey = dkey_sum.astype(jnp.bfloat16)
    dval = dval_sum.astype(jnp.bfloat16)
    grad_part = jnp.einsum("rc,dc->rd", dquery, wq_cols, preferred_element_type=jnp.float32)
    grad_part = grad_part + jnp.einsum(
        "rc,dc->rd", dkey, wk_cols, preferred_element_type=jnp.float32
    )
    grad_part = grad_part + jnp.einsum(
        "rc,dc->rd", dval, wv_cols, preferred_element_type=jnp.float32
    )
    grad_normed = lax.psum(grad_part.astype(jnp.bfloat16), "seq").astype(jnp.float32)
    scaled = grad_normed * gain
    mean_scaled = jnp.mean(scaled, axis=1, keepdims=True)
    scaled_share = lax.dynamic_slice_in_dim(scaled, first_col, col_count, 1)
    share_dot = jnp.sum(scaled_share * unit_share, axis=1, keepdims=True)
    full_unit_dot = lax.psum(share_dot, "seq")
    d_pooled = inv_std * (scaled_share - mean_scaled - unit_share * full_unit_dot / width)
    d_pooled = d_pooled.astype(jnp.bfloat16).reshape(row_count, head_count, HD)
    d_summary = jnp.einsum(
        "rhe,dhe->rhd", d_pooled, value_heads, preferred_element_type=jnp.float32
    ).astype(jnp.bfloat16)
    returned = lax.all_to_all(d_summary, "seq", split_axis=0, concat_axis=1, tiled=True)
    dmix = jnp.einsum("vrd,rhd->vrh", grouped, returned, preferred_element_type=jnp.float32)
    dscore = (mixw * (dmix - jnp.sum(mixw * dmix, axis=0, keepdims=True)) * factor).astype(
        jnp.bfloat16
    )
    grad_tok = jnp.einsum("vrh,rhd->vrd", mix_b, returned, preferred_element_type=jnp.float32)
    grad_tok = grad_tok + jnp.einsum(
        "vrh,hd->vrd", dscore, agg_query, preferred_element_type=jnp.float32
    )
    d_tokens = lax.all_to_all(
        grad_tok.astype(jnp.bfloat16), "var", split_axis=0, concat_axis=1, tiled=True
    )
    query_part = jnp.einsum("vrh,vrd->hd", dscore, grouped, preferred_element_type=jnp.float32)
    d_query = lax.psum(query_part, ("var", "seq"))
    return (attended, d_tokens, d_query)


def solution(mesh):
    return jax.shard_map(
        per_device,
        mesh=mesh,
        in_specs=(
            P("var", "seq", None),
            P(),
            P("var", "seq"),
            P("var", "seq"),
            P("var", "seq"),
            P("var", "seq"),
            P(),
            P(None, "var", "seq"),
        ),
        out_specs=(P(None, "var", "seq"), P("var", "seq", None), P()),
        check_vma=False,
    )
```

profile of v0, /device:TPU:1, one launch (start us, length us, event | category | flops | bytes accessed | tf_op | source)
XLA Modules:
  0.0 1045.8 jit_solution(16454326584296397048)
XLA Ops:
  7.2 2.8 copy.45
  10.0 60.4 %all_to_all.69 = bf16[3,64,4096]{2,0,1:T(4,128)(2,1)S(1)} all-to-all(bf16[3,64,4096]{2,0,1:T(4,128)(2,1)S(1)} %copy.45), channel_id=1, replica_groups=mesh['var'=16,'seq'=32] {'var'}, dimensions={1} | all-to-all | bytes 3145728 | tf_op jit(solution)/shard_map/all_to_all | solution.py:14
  70.4 1.6 copy.46
  72.0 1.0 convolution_multiply_fusion.1
  73.1 0.7 fusion.50
  73.7 2.1 convolution_convert_fusion.1
  75.8 1.8 copy.49
  77.6 11.9 %all-to-all-start.1 = ((bf16[4,32,4096]{2,0,1:T(4,128)(2,1)}), bf16[4,32,4096]{2,0,1:T(4,128)(2,1)S(1)}, u32[]{:S(2)}, u32[]{:S(2)}) async-start(bf16[4,32,4096]{2,0,1:T(4,128)(2,1)} %copy.49), calls=%async_computation.1 | async-start | bytes 2097152 | tf_op jit(solution)/shard_map/all_to_all | solution.py:23
  89.6 0.7 all-gather.6.cloned.1.call-update
  90.4 27.3 %all-to-all-done.1 = bf16[4,32,4096]{2,0,1:T(4,128)(2,1)S(1)} async-done(((bf16[4,32,4096]{2,0,1:T(4,128)(2,1)}), bf16[4,32,4096]{2,0,1:T(4,128)(2,1)S(1)}, u32[]{:S(2)}, u32[]{:S(2)}) %all-to-all-start.1) | async-done | bytes 1048608 | tf_op jit(solution)/shard_map/all_to_all | solution.py:23
  118.0 12.6 %all-gather.6.cloned.1.call-done = bf16[4096,128]{1,0:T(8,128)(2,1)} async-done(((bf16[256,128]{1,0:T(8,128)(2,1)}), bf16[4096,128]{1,0:T(8,128)(2,1)}) %all-gather.6.cloned.1.call-update) | async-done | bytes 1048592 | tf_op jit(solution)/shard_map/all_gather | solution.py:26
  130.6 2.3 convolution_convert_fusion.9
  132.9 0.7 all-gather.14.cloned.1.call-update
  133.7 0.5 all-gather.12.cloned.1.call-update
  134.2 0.5 all-gather.10.cloned.1.call-update
  134.8 71.0 %all-gather.8.cloned.1.call-done = bf16[128,4096]{1,0:T(8,128)(2,1)} async-done(((bf16[128,128]{1,0:T(8,128)(2,1)}), bf16[128,4096]{1,0:T(8,128)(2,1)}) %all-gather.8.cloned.1.call-update) | async-done | bytes 1048592 | tf_op jit(solution)/shard_map/all_gather | solution.py:31
  205.9 1.5 convert_reduce_fusion
  207.4 1.7 fusion.7
  209.1 42.9 %all-gather.14.cloned.1.call-done = bf16[4096,128]{1,0:T(8,128)(2,1)} async-done(((bf16[256,128]{1,0:T(8,128)(2,1)}), bf16[4096,128]{1,0:T(8,128)(2,1)}) %all-gather.14.cloned.1.call-update) | async-done | bytes 1048592 | tf_op jit(solution)/shard_map/all_gather | solution.py:41
  252.0 1.8 convolution_convert_fusion.6
  253.8 17.2 %all_gather.27 = bf16[2048,128]{1,0:T(8,128)(2,1)S(1)} all-gather(bf16[128,128]{1,0:T(8,128)(2,1)S(1)} %convolution_convert_fusion.6), channel_id=1, replica_groups=mesh['var'=16,'seq'=32] {'var'}, dimensions={0}, use_global_device_ids=true | all-gather | bytes 557056 | tf_op jit(solution)/shard_map/all_gather | solution.py:48
  271.0 22.9 %all-gather.12.cloned.1.call-done = bf16[4096,128]{1,0:T(8,128)(2,1)} async-done(((bf16[256,128]{1,0:T(8,128)(2,1)}), bf16[4096,128]{1,0:T(8,128)(2,1)}) %all-gather.12.cloned.1.call-update) | async-done | bytes 1048592 | tf_op jit(solution)/shard_map/all_gather | solution.py:40
  293.9 1.8 convolution_convert_fusion.7
  295.7 17.4 %all_gather.25 = bf16[2048,128]{1,0:T(8,128)(2,1)S(1)} all-gather(bf16[128,128]{1,0:T(8,128)(2,1)S(1)} %convolution_convert_fusion.7), channel_id=1, replica_groups=mesh['var'=16,'seq'=32] {'var'}, dimensions={0}, use_global_device_ids=true | all-gather | bytes 557056 | tf_op jit(solution)/shard_map/all_gather | solution.py:47
  313.0 22.7 %all-gather.10.cloned.1.call-done = bf16[4096,128]{1,0:T(8,128)(2,1)} async-done(((bf16[256,128]{1,0:T(8,128)(2,1)}), bf16[4096,128]{1,0:T(8,128)(2,1)}) %all-gather.10.cloned.1.call-update) | async-done | bytes 1048592 | tf_op jit(solution)/shard_map/all_gather | solution.py:39
  335.8 1.8 convolution_convert_fusion.8
  337.6 0.4 fusion.51
  338.3 0.4 multiply_reduce_fusion
  338.7 0.4 multiply_convert_fusion.1
  339.2 0.8 copy-done.8
  340.0 1.2 convolution_convert_fusion.3
  341.2 1.2 convolution_convert_fusion.2
  342.5 2.2 fusion.14
  344.8 52.4 %reduce-scatter.3.cloned.1.call-done = bf16[128,128]{1,0:T(8,128)(2,1)} async-done(((bf16[2048,128]{1,0:T(8,128)(2,1)}), bf16[128,128]{1,0:T(8,128)(2,1)}) %reduce-scatter.3.cloned.1.call-update) | async-done | bytes 32784 | tf_op jit(solution)/shard_map/reduce_scatter | solution.py:72
  397.1 3.0 convolution_add_fusion.2
  400.1 57.9 %reduce-scatter.5.cloned.1.call-done = bf16[128,128]{1,0:T(8,128)(2,1)} async-done(((bf16[2048,128]{1,0:T(8,128)(2,1)}), bf16[128,128]{1,0:T(8,128)(2,1)}) %reduce-scatter.5.cloned.1.call-update) | async-done | bytes 32784 | tf_op jit(solution)/shard_map/reduce_scatter | solution.py:75
  458.0 3.4 fusion.3
  461.4 1.7 fusion.5
  463.1 155.5 %all-reduce.3.cloned.1.call-done = bf16[128,4096]{1,0:T(8,128)(2,1)} async-done(((bf16[128,4096]{1,0:T(8,128)(2,1)}), bf16[128,4096]{1,0:T(8,128)(2,1)}) %all-reduce.3.cloned.1.call-update) | async-done | bytes 1048592 | tf_op jit(solution)/shard_map/psum | solution.py:88
  618.6 1.6 fusion.25
  620.2 1.3 copy-done.10
  621.5 0.9 multiply_reduce_fusion.2
  622.5 58.5 %psum.22 = f32[128]{0:T(128)S(1)} all-reduce(f32[128]{0:T(128)S(1)} %multiply_reduce_fusion.2), channel_id=1, replica_groups=mesh['var'=16,'seq'=32] {'seq'}, use_global_device_ids=true, to_apply=%region_12.0 | all-reduce | flops 128 | bytes 1024 | tf_op jit(solution)/shard_map/psum | solution.py:93
  681.0 1.4 fusion.4
  682.3 0.6 broadcast.58
  682.9 1.5 reduce.1
  684.4 0.8 reshape.58
  685.2 20.1 %all_to_all.70 = bf16[32,2,8192]{2,1,0:T(2,128)(2,1)S(1)} all-to-all(bf16[32,2,8192]{2,1,0:T(2,128)(2,1)S(1)} %reshape.58), channel_id=1, replica_groups=mesh['var'=16,'seq'=32] {'seq'}, dimensions={0} | all-to-all | bytes 2097152 | tf_op jit(solution)/shard_map/all_to_all | solution.py:99
  705.3 1.0 reshape.59
  706.4 6.4 reduce
  712.8 1.2 all_to_all.58
  714.0 0.5 copy-done.5
  714.5 3.3 convolution_bitcast_fusion.3
  717.8 2.9 convolution_bitcast_fusion
  720.7 2.9 fusion.2
  723.6 3.8 copy.54
  727.4 30.1 %all-to-all-start.3 = ((bf16[48,4,4096]{2,1,0:T(4,128)(2,1)}), bf16[48,4,4096]{2,1,0:T(4,128)(2,1)}, u32[]{:S(2)}, u32[]{:S(2)}) async-start(bf16[48,4,4096]{2,1,0:T(4,128)(2,1)} %copy.54), calls=%async_computation.5 | async-start | bytes 3145728 | tf_op jit(solution)/shard_map/all_to_all | solution.py:108
  757.6 2.9 convolution_bitcast_fusion.1
  760.5 1.0 convolution_convert_fusion.5
  761.5 34.9 %all-to-all-done.3 = bf16[48,4,4096]{2,1,0:T(4,128)(2,1)} async-done(((bf16[48,4,4096]{2,1,0:T(4,128)(2,1)}), bf16[48,4,4096]{2,1,0:T(4,128)(2,1)}, u32[]{:S(2)}, u32[]{:S(2)}) %all-to-all-start.3) | async-done | bytes 1572896 | tf_op jit(solution)/shard_map/all_to_all | solution.py:108
  796.4 2.1 copy.55
  798.5 1.8 all_to_all.64
  800.3 237.1 %all-reduce.5.cloned.1.call-done = f32[32,4096]{1,0:T(8,128)} async-done(((f32[32,4096]{1,0:T(8,128)}), f32[32,4096]{1,0:T(8,128)}) %all-reduce.5.cloned.1.call-update) | async-done | bytes 524304 | tf_op jit(solution)/shard_map/psum | solution.py:112
  1037.4 1.9 copy.78
  (56 shorter events, 1.1 us)
Async XLA Ops:
  7.2 64.8 %copy-start = (bf16[32,4096]{1,0:T(8,128)(2,1)S(1)}, bf16[32,4096]{1,0:T(8,128)(2,1)}, u32[]{:S(2)}) copy-start(bf16[32,4096]{1,0:T(8,128)(2,1)} %param.9) | copy-start | bytes 786436
  72.0 3.8 copy-start.4
  77.6 40.0 %all-to-all-start.1 = ((bf16[4,32,4096]{2,0,1:T(4,128)(2,1)}), bf16[4,32,4096]{2,0,1:T(4,128)(2,1)S(1)}, u32[]{:S(2)}, u32[]{:S(2)}) async-start(bf16[4,32,4096]{2,0,1:T(4,128)(2,1)} %copy.49), calls=%async_computation.1 | async-start | bytes 2097152 | tf_op jit(solution)/shard_map/all_to_all | solution.py:23
  89.6 41.0 %all-gather.6.cloned.1.call-start = ((), (), s32[]{:S(2)}) async-start(), calls=%async_computation.6 | async-start | bytes 1114112 | tf_op jit(solution)/shard_map/all_gather | solution.py:26
  90.3 115.5 %all-gather.8.cloned.1.call-start = ((), (), s32[]{:S(2)}) async-start(), calls=%async_computation.7 | async-start | bytes 1081344 | tf_op jit(solution)/shard_map/all_gather | solution.py:31
  117.9 134.0 %copy-start.13 = (f32[4096]{0:T(1024)S(1)}, f32[4096]{0:T(1024)}, u32[]{:S(2)}) copy-start(f32[4096]{0:T(1024)} %param.14) | copy-start | bytes 49156
  132.9 119.1 %all-gather.14.cloned.1.call-start = ((), (), s32[]{:S(2)}) async-start(), calls=%async_computation.10 | async-start | bytes 1114112 | tf_op jit(solution)/shard_map/all_gather | solution.py:41
  133.6 160.3 %all-gather.12.cloned.1.call-start = ((), (), s32[]{:S(2)}) async-start(), calls=%async_computation.9 | async-start | bytes 1114112 | tf_op jit(solution)/shard_map/all_gather | solution.py:40
  134.2 201.6 %all-gather.10.cloned.1.call-start = ((), (), s32[]{:S(2)}) async-start(), calls=%async_computation.8 | async-start | bytes 1114112 | tf_op jit(solution)/shard_map/all_gather | solution.py:39
  134.8 262.3 %reduce-scatter.3.cloned.1.call-start = ((), (), s32[]{:S(2)}) async-start(), calls=%async_computation.11 | async-start | bytes 557056 | tf_op jit(solution)/shard_map/reduce_scatter | solution.py:72
  205.9 46.1 %copy-start.3 = (bf16[128,4096]{1,0:T(8,128)(2,1)S(1)}, bf16[128,4096]{1,0:T(8,128)(2,1)}, u32[]{:S(2)}) copy-start(bf16[128,4096]{1,0:T(8,128)(2,1)} %all-gather.8.cloned.1.call-done) | copy-start | bytes 3145732
  253.8 82.0 %copy-start.14 = (f32[4096]{0:T(1024)S(1)}, f32[4096]{0:T(1024)}, u32[]{:S(2)}) copy-start(f32[4096]{0:T(1024)} %param.14) | copy-start | bytes 49156
  271.0 67.3 %copy-start.11 = (bf16[2048,128]{1,0:T(8,128)(2,1)}, bf16[2048,128]{1,0:T(8,128)(2,1)S(1)}, u32[]{:S(2)}) copy-start(bf16[2048,128]{1,0:T(8,128)(2,1)S(1)} %all_gather.27) | copy-start | bytes 1572868
  313.0 24.9 %copy-start.7 = (bf16[2048,128]{1,0:T(8,128)(2,1)}, bf16[2048,128]{1,0:T(8,128)(2,1)S(1)}, u32[]{:S(2)}) copy-start(bf16[2048,128]{1,0:T(8,128)(2,1)S(1)} %all_gather.25) | copy-start | bytes 1572868
  337.6 0.8 copy-start.18
  338.0 3.2 copy-start.1
  338.3 2.9 copy-start.16
  338.7 2.5 copy-start.19
  339.1 0.8 copy-start.8
  341.1 116.9 %reduce-scatter.5.cloned.1.call-start = ((), (), s32[]{:S(2)}) async-start(), calls=%async_computation.12 | async-start | bytes 557056 | tf_op jit(solution)/shard_map/reduce_scatter | solution.py:75
  342.5 276.1 %all-reduce.3.cloned.1.call-start = ((), (), s32[]{:S(2)}) async-start(), calls=%async_computation.13 | async-start | bytes 2097152 | tf_op jit(solution)/shard_map/psum | solution.py:88
  461.4 157.2 %copy-start.15 = (f32[4096]{0:T(1024)S(1)}, f32[4096]{0:T(1024)}, u32[]{:S(2)}) copy-start(f32[4096]{0:T(1024)} %param.14) | copy-start | bytes 49156
  463.1 217.8 %copy-start.9 = (bf16[4096,128]{1,0:T(8,128)(2,1)S(1)}, bf16[4096,128]{1,0:T(8,128)(2,1)}, u32[]{:S(2)}) copy-start(bf16[4096,128]{1,0:T(8,128)(2,1)} %all-gather.6.cloned.1.call-done) | copy-start | bytes 3145732
  620.2 1.3 copy-start.10
  712.7 1.8 copy-start.5
  727.4 30.2 %copy-start.6 = (bf16[3,16,4,4096]{3,2,0,1:T(4,128)(2,1)S(1)}, bf16[3,16,4,4096]{3,2,0,1:T(4,128)(2,1)}, u32[]{:S(2)}) copy-start(bf16[3,16,4,4096]{3,2,0,1:T(4,128)(2,1)} %copy-done.4) | copy-start | bytes 4718596
  727.4 69.0 %all-to-all-start.3 = ((bf16[48,4,4096]{2,1,0:T(4,128)(2,1)}), bf16[48,4,4096]{2,1,0:T(4,128)(2,1)}, u32[]{:S(2)}, u32[]{:S(2)}) async-start(bf16[48,4,4096]{2,1,0:T(4,128)(2,1)} %copy.54), calls=%async_computation.5 | async-start | bytes 3145728 | tf_op jit(solution)/shard_map/all_to_all | solution.py:108
  757.5 3.0 copy-start.2
  757.5 3.0 copy-start.12
  757.5 3.0 copy-start.17
  757.5 279.9 %all-reduce.5.cloned.1.call-start = ((), (), s32[]{:S(2)}) async-start(), calls=%async_computation.14 | async-start | bytes 1048576 | tf_op jit(solution)/shard_map/psum | solution.py:112
Sparse Core Ops, SparseCore 0:
  92.5 37.9 all-gather.5
  134.2 71.6 all-gather.7
  208.0 43.9 all-gather.13
  254.0 39.8 all-gather.11
  295.9 39.8 all-gather.9
  341.3 55.7 reduce-scatter.2
  400.1 57.8 reduce-scatter.4
  461.5 157.0 all-reduce.2
  763.3 274.0 all-reduce.4
where the time goes:
time: 1050 us
  waiting for transfers between devices  740 us (70%)
  blocking collectives  174 us (17%)
  starting transfers between devices  42.4 us (4%)
  matrix products  36.8 us (4%)
  local copies, waits for them, and re-layouts  22.5 us (2%)
  other arithmetic  16.7 us (2%)
  between operations  14.2 us (1%)
    psum x1, waiting for transfers between devices, per_device(): d_query = lax.psum(query_part, ('var', 'seq'))  237 us
    psum x1, waiting for transfers between devices, per_device(): lax.psum(grad_part.astype(jnp.bfloat16), 'seq').astype(jnp.float32)  155 us
    all_gather x1, waiting for transfers between devices, per_device(): lax.all_gather(pooled, 'seq', axis=1, tiled=True).astype(jnp.float32)  71 us
    all_to_all x1, blocking collectives, per_device(): lax.all_to_all(tokens, 'var', split_axis=1, concat_axis=0, tiled=True)  60.4 us
    psum x1, blocking collectives, per_device(): full_unit_dot = lax.psum(share_dot, 'seq')  58.5 us
    reduce_scatter x1, waiting for transfers between devices, per_device(): lax.psum_scatter(dvals[0].astype(jnp.bfloat16), 'var', scatter_dimension=...  57.9 us
    reduce_scatter x1, waiting for transfers between devices, per_device(): lax.psum_scatter(dkeys[0].astype(jnp.bfloat16), 'var', scatter_dimension=...  52.4 us
    all_gather x1, waiting for transfers between devices, per_device(): lax.all_gather(w_value, 'var', axis=0, tiled=True)  42.9 us
  transfers between devices with their start and end apart: 11, of which 11 were waited for; matrix products, arithmetic and copies ran while one was open for 2% of the time, Pallas kernels for 0%

commit v1 on v0

v1 whole, which is shorter than its diff:
```python
import functools

import jax
import jax.numpy as jnp
from jax import lax
from jax.experimental import pallas as pl
from jax.experimental.pallas import tpu as pltpu
from jax.sharding import PartitionSpec as P

HD = 128
EPS = 1e-05
NZ = 8
MESH = pl.DeviceIdType.MESH
F32 = jnp.float32
BF16 = jnp.bfloat16


def remote(src, dst, send, recv, device):
    return pltpu.make_async_remote_copy(
        src_ref=src, dst_ref=dst, send_sem=send, recv_sem=recv, device_id=device, device_id_type=MESH
    )


def loop(first, last, body):
    def step(k, carry):
        body(k)
        return carry

    lax.fori_loop(first, last, step, 0)


def slot(ref, j):
    return ref.at[j]


def whole(ref, j):
    return ref


class Direct:
    def __init__(self, axis, n, src=slot, dst=slot):
        self.axis, self.n, self.src, self.dst = axis, n, src, dst

    def sems(self):
        return [pltpu.SemaphoreType.DMA((self.n,)), pltpu.SemaphoreType.DMA((self.n,)), pltpu.SemaphoreType.DMA(())]

    def peers(self):
        me = lax.axis_index(self.axis)
        return [(self.n - 1, lambda k: {self.axis: lax.rem(me + k + 1, self.n)})]

    def kinds(self):
        return [self.axis]

    def own(self, x, o, sems):
        me = lax.axis_index(self.axis)
        return pltpu.make_async_copy(self.src(x, me), self.dst(o, me), sems[2])

    def start(self, x, o, sems):
        me = lax.axis_index(self.axis)

        def send(k):
            to = lax.rem(me + k, self.n)
            remote(self.src(x, to), self.dst(o, me), sems[0].at[k], sems[1].at[k], {self.axis: to}).start()

        loop(1, self.n, send)
        self.own(x, o, sems).start()

    def middle(self, x, o, sems):
        pass

    def finish(self, x, o, sems):
        me = lax.axis_index(self.axis)
        self.own(x, o, sems).wait()

        def wait(k):
            to, source = lax.rem(me + k, self.n), lax.rem(me + self.n - k, self.n)
            remote(self.src(x, to), self.dst(o, source), sems[0].at[k], sems[1].at[k], {self.axis: to}).wait()

        loop(1, self.n, wait)


class GatherSeq:
    def __init__(self, n):
        self.nz = NZ
        self.nx = n // NZ

    def sems(self):
        dma = pltpu.SemaphoreType.DMA
        return [dma((self.nz,)), dma((self.nz,)), dma((self.nz, self.nx)), dma((self.nz, self.nx)), dma(())]

    def place(self):
        me = lax.axis_index("seq")
        return me, me // self.nz, lax.rem(me, self.nz)

    def peers(self):
        me, x, z = self.place()
        return [
            (self.nz - 1, lambda k: {"seq": x * self.nz + lax.rem(z + k + 1, self.nz)}),
            (self.nx - 1, lambda k: {"seq": lax.rem(x + k + 1, self.nx) * self.nz + z}),
        ]

    def kinds(self):
        return ["z", "x"]

    def along_z(self, a, o, sems, k, received):
        me, x, z = self.place()
        at = lax.rem(z + self.nz - k, self.nz) if received else z
        return remote(
            a, o.at[x * self.nz + at], sems[0].at[k], sems[1].at[k],
            {"seq": x * self.nz + lax.rem(z + k, self.nz)},
        )

    def along_x(self, o, sems, k, m, received):
        me, x, z = self.place()
        zz = lax.rem(z + self.nz - k, self.nz)
        src = o.at[x * self.nz + zz]
        row = lax.rem(x + self.nx - m, self.nx) if received else x
        return remote(
            src, o.at[row * self.nz + zz], sems[2].at[k, m], sems[3].at[k, m],
            {"seq": lax.rem(x + m, self.nx) * self.nz + z},
        )

    def start(self, a, o, sems):
        me, x, z = self.place()
        pltpu.make_async_copy(a, o.at[me], sems[4]).start()
        loop(1, self.nz, lambda k: self.along_z(a, o, sems, k, False).start())

    def middle(self, a, o, sems):
        me, x, z = self.place()
        pltpu.make_async_copy(a, o.at[me], sems[4]).wait()
        loop(1, self.nx, lambda m: self.along_x(o, sems, 0, m, False).start())

        def forward(k):
            self.along_z(a, o, sems, k, True).wait_recv()
            loop(1, self.nx, lambda m: self.along_x(o, sems, k, m, False).start())

        loop(1, self.nz, forward)

    def finish(self, a, o, sems):
        loop(1, self.nz, lambda k: self.along_z(a, o, sems, k, False).wait_send())

        def wait(k):
            loop(1, self.nx, lambda m: self.along_x(o, sems, k, m, True).wait())

        loop(0, self.nz, wait)


class GatherVar:
    def __init__(self, n, dst=slot, ring=False):
        self.n, self.ny, self.dst, self.ring = n, n // 2, dst, ring
        self.right = self.ny // 2
        self.left = (self.ny - 1) // 2

    def sems(self):
        dma = pltpu.SemaphoreType.DMA
        return [dma((self.ny,)), dma((self.ny,)), dma((self.ny,)), dma((self.ny,)), dma(())]

    def place(self):
        me = lax.axis_index("var")
        return me, me // 2, lax.rem(me, 2)

    def peers(self):
        me, y, c = self.place()
        across = (1, lambda k: {"var": 2 * y + 1 - c})
        if self.ring:
            near = [(1, lambda k: {"var": 2 * lax.rem(y + 1, self.ny) + c})]
            if self.ny > 2:
                near.append((1, lambda k: {"var": 2 * lax.rem(y + self.ny - 1, self.ny) + c}))
            return near + [across]
        return [(self.ny - 1, lambda k: {"var": 2 * lax.rem(y + k + 1, self.ny) + c}), across]

    def kinds(self):
        return (["y1", "y-1", "core"] if self.ny > 2 else ["y1", "core"]) if self.ring else ["y", "core"]

    def along_y(self, a, o, sems, k, received):
        me, y, c = self.place()
        at = 2 * lax.rem(y + self.ny - k, self.ny) + c if received else me
        return remote(
            a, self.dst(o, at), sems[0].at[k], sems[1].at[k], {"var": 2 * lax.rem(y + k, self.ny) + c}
        )

    def hop(self, a, o, sems, t, way, received):
        me, y, c = self.place()
        k = t if way == 1 else self.ny - t
        behind = t - 1 if not received else t
        at = 2 * lax.rem(y + self.ny * 2 - way * behind, self.ny) + c
        src = a if (isinstance(t, int) and t == 1 and not received) else self.dst(o, at)
        return remote(
            src, self.dst(o, at), sems[0].at[k], sems[1].at[k], {"var": 2 * lax.rem(y + self.ny + way, self.ny) + c}
        )

    def across(self, o, sems, k, received, first=None):
        me, y, c = self.place()
        side = 1 - c if received else c
        at = 2 * lax.rem(y + self.ny - k, self.ny) + side
        src = self.dst(o, at) if first is None else first
        return remote(src, self.dst(o, at), sems[2].at[k], sems[3].at[k], {"var": 2 * y + 1 - c})

    def own(self, a, o, sems):
        return pltpu.make_async_copy(a, self.dst(o, lax.axis_index("var")), sems[4])

    def start(self, a, o, sems):
        if self.ring:
            self.hop(a, o, sems, 1, 1, False).start()
            if self.left:
                self.hop(a, o, sems, 1, -1, False).start()
        else:
            loop(1, self.ny, lambda k: self.along_y(a, o, sems, k, False).start())
        self.across(o, sems, 0, False, a).start()
        self.own(a, o, sems).start()

    def middle(self, a, o, sems):
        if self.ring:
            for t in range(1, self.right + 1):
                self.hop(a, o, sems, t, 1, True).wait_recv()
                if t < self.right:
                    self.hop(a, o, sems, t + 1, 1, False).start()
                self.across(o, sems, t, False).start()
                if t <= self.left:
                    self.hop(a, o, sems, t, -1, True).wait_recv()
                    if t < self.left:
                        self.hop(a, o, sems, t + 1, -1, False).start()
                    self.across(o, sems, self.ny - t, False).start()
        else:
            def forward(k):
                self.along_y(a, o, sems, k, True).wait_recv()
                self.across(o, sems, k, False).start()

            loop(1, self.ny, forward)

    def finish(self, a, o, sems):
        self.own(a, o, sems).wait()
        if self.ring:
            for t in range(1, self.right + 1):
                self.hop(a, o, sems, t, 1, False).wait_send()
                if t <= self.left:
                    self.hop(a, o, sems, t, -1, False).wait_send()
        else:
            loop(1, self.ny, lambda k: self.along_y(a, o, sems, k, False).wait_send())
        self.across(o, sems, 0, False, a).wait_send()
        self.across(o, sems, 0, True).wait_recv()

        def wait(k):
            self.across(o, sems, k, False).wait_send()
            self.across(o, sems, k, True).wait_recv()

        loop(1, self.ny, wait)


def barrier(jobs):
    groups = {}
    for job in jobs:
        for kind, group in zip(job.kinds(), job.peers()):
            groups[kind] = group
    if "seq" in groups:
        groups.pop("z", None), groups.pop("x", None)
    if "var" in groups:
        for kind in ("y", "y1", "y-1", "core"):
            groups.pop(kind, None)
    if "y" in groups:
        groups.pop("y1", None), groups.pop("y-1", None)
    sem = pltpu.get_barrier_semaphore()
    total = 0
    for count, to in groups.values():
        def greet(k, to=to):
            pl.semaphore_signal(sem, inc=1, device_id=to(k), device_id_type=MESH)

        loop(0, count, greet)
        total += count
    pl.semaphore_wait(sem, total)


def exchange(name, cid, jobs, arrays, outs):
    n = len(jobs)
    counts = [len(job.sems()) for job in jobs]

    def kernel(*refs):
        xs, os, rest = refs[:n], refs[n : 2 * n], list(refs[2 * n :])
        sems = []
        for count in counts:
            sems.append(rest[:count])
            rest = rest[count:]
        barrier(jobs)
        for phase in ("start", "middle", "finish"):
            for job, x, o, s in zip(jobs, xs, os, sems):
                getattr(job, phase)(x, o, s)

    return pl.pallas_call(
        kernel,
        name=name,
        out_shape=[jax.ShapeDtypeStruct(*out) for out in outs],
        in_specs=[pl.BlockSpec(memory_space=pl.ANY)] * n,
        out_specs=[pl.BlockSpec(memory_space=pl.ANY)] * n,
        scratch_shapes=[sem for job in jobs for sem in job.sems()],
        compiler_params=pltpu.CompilerParams(collective_id=cid, has_side_effects=True),
    )(*arrays)


def sum_seq(q_ref, z_held, x_held, done, sems, nx, nz):
    me = lax.axis_index("seq")
    x, z = me // nz, lax.rem(me, nz)

    def swap(src, held, place, n, device, sem):
        own = pltpu.make_async_copy(src, held.at[place], sem[2])
        own.start()

        def copy(k, received):
            at = lax.rem(place + n - k, n) if received else place
            return remote(src, held.at[at], sem[0].at[k], sem[1].at[k], device(lax.rem(place + k, n)))

        loop(1, n, lambda k: copy(k, False).start())
        own.wait()
        loop(1, n, lambda k: copy(k, True).wait())
        total = held[0]
        for at in range(1, n):
            total = total + held[at]
        done[...] = total

    swap(q_ref, z_held, z, nz, lambda k: {"seq": x * nz + k}, sems[:3])
    swap(done, x_held, x, nx, lambda k: {"seq": k * nz + z}, sems[3:])


def tokens_back(cid, d_tok, q_part, n_var, n_seq):
    nz, nx = NZ, n_seq // NZ
    _, per, rows, cols = d_tok.shape
    back = Direct("var", n_var, slot, lambda o, j: o.at[:, :, pl.ds(pl.multiple_of(j * cols, cols), cols)])
    spread = GatherVar(n_var, lambda o, j: o.at[:, pl.ds(pl.multiple_of(j * cols, cols), cols)])
    dma = pltpu.SemaphoreType.DMA

    def kernel(t_ref, q_ref, dt_ref, dq_ref, z_held, x_held, done, *sems):
        me = lax.axis_index("seq")
        x, z = me // nz, lax.rem(me, nz)

        barrier([back, GatherSeq(n_seq)])
        back_sems, spread_sems, sum_sems = sems[:3], sems[3:8], sems[8:]
        back.start(t_ref, dt_ref, back_sems)
        sum_seq(q_ref, z_held, x_held, done, sum_sems, nx, nz)
        spread.start(done, dq_ref, spread_sems)
        spread.middle(done, dq_ref, spread_sems)
        spread.finish(done, dq_ref, spread_sems)
        back.finish(t_ref, dt_ref, back_sems)

    heads = q_part.shape[0]
    return pl.pallas_call(
        kernel,
        name="tokens_back",
        out_shape=[
            jax.ShapeDtypeStruct((per, rows, cols * n_var), BF16),
            jax.ShapeDtypeStruct((heads, cols * n_var), F32),
        ],
        in_specs=[pl.BlockSpec(memory_space=pl.ANY)] * 2,
        out_specs=[pl.BlockSpec(memory_space=pl.ANY)] * 2,
        scratch_shapes=[
            pltpu.VMEM((nz, heads, cols), F32),
            pltpu.VMEM((nx, heads, cols), F32),
            pltpu.VMEM((heads, cols), F32),
            *back.sems(),
            *spread.sems(),
            dma((nz,)), dma((nz,)), dma(()), dma((nx,)), dma((nx,)), dma(()),
        ],
        compiler_params=pltpu.CompilerParams(collective_id=cid, has_side_effects=True),
    )(d_tok, q_part)


def per_device(n_var, n_seq, tokens, agg_query, agg_value, w_query, w_key, w_value, gain, d_out):
    factor = HD ** (-0.5)
    per, rows, width = tokens.shape
    heads = agg_query.shape[0]
    n_vars = per * n_var
    cut = width // n_var
    own = rows // n_var
    line = own * heads
    i = lax.axis_index("var")

    local_scores = jnp.einsum("vpd,hd->vph", tokens, agg_query, preferred_element_type=F32) * factor
    flat = per * rows * heads // 128
    grouped, scores, value = exchange(
        "tokens_out",
        0,
        [
            Direct("var", n_var, lambda x, j: x.at[:, :, pl.ds(pl.multiple_of(j * cut, cut), cut)], slot),
            GatherVar(n_var),
            GatherSeq(n_seq),
        ],
        [tokens, local_scores.reshape(flat, 128), agg_value],
        [
            ((n_var, per, rows, cut), BF16),
            ((n_var, flat, 128), F32),
            ((n_seq, cut, HD), BF16),
        ],
    )
    grouped = grouped.reshape(n_vars, rows, cut)
    mixw = jax.nn.softmax(scores.reshape(n_vars, rows, heads), axis=0)
    mix_b = mixw.astype(BF16)
    summary = jnp.einsum("vph,vpd->phd", mix_b, grouped, preferred_element_type=F32).astype(BF16)
    pooled_part = jnp.einsum("phd,hde->phe", summary, value, preferred_element_type=F32).astype(BF16)
    (pooled_in,) = exchange(
        "pooled_sum",
        1,
        [Direct("var", n_var)],
        [pooled_part.reshape(n_var, line, HD)],
        [((n_var, line, HD), BF16)],
    )
    pooled = jnp.sum(pooled_in.astype(F32), axis=0).astype(BF16).astype(F32).reshape(own, heads, HD)
    gain3 = gain.reshape(1, heads, HD)
    center = jnp.mean(pooled, axis=(1, 2), keepdims=True)
    spread = jnp.mean((pooled - center) ** 2, axis=(1, 2), keepdims=True)
    inv_std = lax.rsqrt(spread + EPS)
    unit = (pooled - center) * inv_std
    normed = (unit * gain3).astype(BF16)
    weights = jnp.concatenate([w_query, w_key, w_value], axis=1)
    normed_all, weights_all = exchange(
        "normed_out",
        2,
        [GatherSeq(n_seq), GatherVar(n_var, ring=True)],
        [normed.reshape(line, HD), weights],
        [((n_seq, line, HD), BF16), ((n_var, cut, 3 * HD), BF16)],
    )
    weights_all = weights_all.reshape(width, 3 * HD)
    row_count = n_seq * own
    normed_rows = normed_all.reshape(row_count, width)
    qkv = jnp.dot(normed_rows, weights_all, preferred_element_type=F32).astype(BF16)
    queries = qkv[:, :HD]
    (kv,) = exchange(
        "keys_values",
        3,
        [GatherVar(n_var)],
        [qkv[:, HD:]],
        [((n_var, row_count, 2 * HD), BF16)],
    )
    kv = kv.reshape(n_var * row_count, 2 * HD)
    all_keys, all_values = kv[:, :HD], kv[:, HD:]
    grad_out = d_out.reshape(row_count, HD)
    logits = jnp.einsum("qe,ke->qk", queries, all_keys, preferred_element_type=F32) * factor
    top = jnp.max(logits, axis=1, keepdims=True)
    expo = jnp.exp(logits - top)
    probs = expo / jnp.sum(expo, axis=1, keepdims=True)
    probs_b = probs.astype(BF16)
    attended = jnp.dot(probs_b, all_values, preferred_element_type=F32).astype(BF16)
    dprob = jnp.einsum("qe,ke->qk", grad_out, all_values, preferred_element_type=F32)
    inner = jnp.sum(probs * dprob, axis=1, keepdims=True)
    dlogit = (probs * (dprob - inner) * factor).astype(BF16)
    dquery = jnp.dot(dlogit, all_keys, preferred_element_type=F32).astype(BF16)
    dkey = jnp.einsum("qk,qe->ke", dlogit, queries, preferred_element_type=F32).astype(BF16)
    dval = jnp.einsum("qk,qe->ke", probs_b, grad_out, preferred_element_type=F32).astype(BF16)
    (dkv_in,) = exchange(
        "keys_values_back",
        4,
        [Direct("var", n_var)],
        [jnp.concatenate([dkey, dval], axis=1).reshape(n_var, row_count, 2 * HD)],
        [((n_var, row_count, 2 * HD), BF16)],
    )
    dkv = jnp.sum(dkv_in.astype(F32), axis=0).astype(BF16)
    dqkv = jnp.concatenate([dquery, dkv], axis=1)
    grad_part = jnp.einsum("rc,dc->rd", dqkv, weights_all, preferred_element_type=F32).astype(BF16)
    (grad_in,) = exchange(
        "normed_back",
        5,
        [Direct("seq", n_seq)],
        [grad_part.reshape(n_seq, line, HD)],
        [((n_seq, line, HD), BF16)],
    )
    grad_normed = jnp.sum(grad_in.astype(F32), axis=0).reshape(own, heads, HD)
    scaled = grad_normed * gain3
    mean_scaled = jnp.mean(scaled, axis=(1, 2), keepdims=True)
    mean_dot = jnp.mean(scaled * unit, axis=(1, 2), keepdims=True)
    d_pooled = (inv_std * (scaled - mean_scaled - unit * mean_dot)).astype(BF16)
    (d_pooled_all,) = exchange(
        "pooled_back",
        6,
        [GatherVar(n_var)],
        [d_pooled.reshape(line, HD)],
        [((n_var, line, HD), BF16)],
    )
    d_pooled_all = d_pooled_all.reshape(rows, heads, HD)
    d_summary = jnp.einsum("phe,hde->phd", d_pooled_all, value, preferred_element_type=F32).astype(BF16)
    dmix_part = jnp.einsum("vpd,phd->pvh", grouped, d_summary, preferred_element_type=F32)
    (dmix_in,) = exchange(
        "dmix_sum",
        7,
        [Direct("var", n_var)],
        [dmix_part.reshape(n_var, flat, 128)],
        [((n_var, flat, 128), F32)],
    )
    dmix = jnp.sum(dmix_in, axis=0).reshape(own, n_vars, heads)
    mix_own = lax.dynamic_slice_in_dim(mixw, i * own, own, 1).transpose(1, 0, 2)
    dscore = (mix_own * (dmix - jnp.sum(mix_own * dmix, axis=1, keepdims=True)) * factor).astype(BF16)
    (dscore_all,) = exchange(
        "dscore_out",
        8,
        [GatherVar(n_var)],
        [dscore.reshape(flat, 128)],
        [((n_var, flat, 128), BF16)],
    )
    dscore_all = dscore_all.reshape(rows, n_vars, heads)
    query_cut = lax.dynamic_slice_in_dim(agg_query, i * cut, cut, 1)
    query_part = jnp.einsum("pvh,vpd->hd", dscore_all, grouped, preferred_element_type=F32)
    grad_tok = jnp.einsum("vph,phd->vpd", mix_b, d_summary, preferred_element_type=F32)
    grad_tok = grad_tok + jnp.einsum("pvh,hd->vpd", dscore_all, query_cut, preferred_element_type=F32)
    d_tokens, d_query = tokens_back(
        9, grad_tok.astype(BF16).reshape(n_var, per, rows, cut), query_part, n_var, n_seq
    )
    return (attended.reshape(d_out.shape), d_tokens, d_query)


def solution(mesh):
    return jax.shard_map(
        functools.partial(per_device, mesh.shape["var"], mesh.shape["seq"]),
        mesh=mesh,
        in_specs=(
            P("var", "seq", None),
            P(),
            P("var", "seq"),
            P("var", "seq"),
            P("var", "seq"),
            P("var", "seq"),
            P(),
            P(None, "var", "seq"),
        ),
        out_specs=(P(None, "var", "seq"), P("var", "seq", None), P()),
        check_vma=False,
    )
```

time: 1050 us -> 380 us (0.36)
  waiting for transfers between devices: 740 us -> 0 us
  Pallas kernels: 0 us -> 309 us
  blocking collectives: 174 us -> 0 us
  starting transfers between devices: 42.4 us -> 0 us
  between operations: 14.2 us -> 1.16 us
    psum x2 -> x0, waiting for transfers between devices: 393 us -> none  [the longest x1 237 us: per_device(): d_query = lax.psum(query_part, ('var', 'seq'))]
    pallas_call x0 -> x10, Pallas kernels: none -> 309 us  [the longest x9 259 us: exchange(): pl.pallas_call(kernel, name=name, out_shape=[jax.ShapeDtypeStruct(*out) f...]
    all_gather x5 -> x0, waiting for transfers between devices: 172 us -> none  [the longest x1 71 us: per_device(): lax.all_gather(pooled, 'seq', axis=1, tiled=True).astype(jnp.float32)]
    reduce_scatter x2 -> x0, waiting for transfers between devices: 110 us -> none  [the longest x1 57.9 us: per_device(): lax.psum_scatter(dvals[0].astype(jnp.bfloat16), 'var', scatter_dimension=...]
    all_to_all x2 -> x0, blocking collectives: 80.5 us -> none  [the longest x1 60.4 us: per_device(): lax.all_to_all(tokens, 'var', split_axis=1, concat_axis=0, tiled=True)]
    all_to_all x2 -> x0, waiting for transfers between devices: 62.2 us -> none  [the longest x1 34.9 us: per_device(): lax.all_to_all(grad_tok.astype(jnp.bfloat16), 'var', split_axis=0, concat...]
    psum x1 -> x0, blocking collectives: 58.5 us -> none  [per_device(): full_unit_dot = lax.psum(share_dot, 'seq')]
    all_to_all x2 -> x0, starting transfers between devices: 42 us -> none  [the longest x1 30.1 us: per_device(): lax.all_to_all(grad_tok.astype(jnp.bfloat16), 'var', split_axis=0, concat...]
  transfers between devices with their start and end apart: 11 -> 0, of which waited for: 11 -> 0; matrix products, arithmetic and copies ran while one was open for 2% -> 0% of each run, Pallas kernels for 0% -> 0%
where the time goes in v1:
time: 380 us; the launch traced here: 378 us
  Pallas kernels  309 us (81%)
  local copies, waits for them, and re-layouts  28.6 us (8%)
  matrix products  26.3 us (7%)
  other arithmetic  13.5 us (4%)
    pallas_call x9, Pallas kernels, exchange(): pl.pallas_call(kernel, name=name, out_shape=[jax.ShapeDtypeStruct(*out) f...  259 us
    pallas_call x1, Pallas kernels, tokens_back(): pl.pallas_call(kernel, name='tokens_back', out_shape=[jax.ShapeDtypeStruc...  49.9 us

profile of v1, /device:TPU:1, one launch (start us, length us, event | category | flops | bytes accessed | tf_op | source)
XLA Modules:
  0.0 378.4 jit_solution(17832719157762496214)
XLA Ops:
  0.6 0.9 copy-done
  1.6 2.1 convolution_multiply_fusion.1
  3.8 0.7 reshape.150.refs_1_
  4.5 74.9 %tokens_out.1 = (bf16[16,3,64,256]{3,2,1,0:T(8,128)(2,1)}, f32[16,48,128]{2,1,0:T(8,128)}, bf16[32,256,128]{2,1,0:T(8,128)(2,1)}) custom-call(bf16[3,64,4096]{2,1,0:T(8,128)(2,1)} %refs_0_.1, f32[48,128]{1,0:T(8,128)} %reshape.150.refs_1_, bf16[256,128]{1,0:T(8,128)(2,1)} %refs_2_.1), custom_call_target="tpu_custom_call" | custom-call | tf_op jit(solution)/shard_map/tokens_out/pallas_call | solution.py:288
  79.4 1.4 reshape.151
  80.8 1.8 copy.44
  82.6 0.1 reduce_max.18
  82.8 1.9 fusion.18
  84.7 1.8 fusion.17
  86.5 1.2 convolution_convert_fusion.4
  87.7 0.7 copy-done.8
  88.5 0.8 fusion.3
  89.3 1.1 copy.47
  90.4 23.9 %pooled_sum.1 = bf16[16,128,128]{2,1,0:T(8,128)(2,1)} custom-call(bf16[16,128,128]{2,1,0:T(8,128)(2,1)} %bitcast.76), custom_call_target="tpu_custom_call" | custom-call | tf_op jit(solution)/shard_map/pooled_sum/pallas_call | solution.py:288
  114.3 1.1 reduce_sum.131
  115.8 0.5 copy-done.25
  116.5 0.2 multiply_reduce_fusion.2
  116.9 0.5 copy-done.27
  117.6 0.7 fusion.37.refs_0_
  118.3 0.7 pad_maximum_fusion.1.refs_1_
  119.0 33.4 %normed_out.1 = (bf16[32,128,128]{2,1,0:T(8,128)(2,1)}, bf16[16,256,384]{2,1,0:T(8,128)(2,1)}) custom-call(bf16[128,128]{1,0:T(8,128)(2,1)} %fusion.37.refs_0_, bf16[256,384]{1,0:T(8,128)(2,1)} %pad_maximum_fusion.1.refs_1_), custom_call_target="tpu_custom_call" | custom-call | tf_op jit(solution)/shard_map/normed_out/pallas_call | solution.py:288
  152.4 2.3 reshape.154
  154.7 2.9 convolution_convert_fusion.6
  157.6 0.6 slice.17.refs_0_
  158.3 21.1 %keys_values.1 = bf16[16,128,256]{2,1,0:T(8,128)(2,1)} custom-call(bf16[128,256]{1,0:T(8,128)(2,1)} %slice.17.refs_0_), custom_call_target="tpu_custom_call" | custom-call | tf_op jit(solution)/shard_map/keys_values/pallas_call | solution.py:288
  179.4 1.5 fusion.53
  180.9 0.3 fusion.20
  181.3 0.4 multiply_reduce_fusion
  181.7 0.2 copy-done.6
  181.9 0.4 multiply_convert_fusion
  182.3 1.0 convolution_convert_fusion.7
  183.3 1.5 copy.50
  184.7 0.3 convolution_convert_fusion.2
  185.1 1.6 convolution_convert_fusion.1
  186.7 1.1 pad_maximum_fusion
  187.8 2.3 copy.49
  190.1 30.7 %keys_values_back.1 = bf16[16,128,256]{2,1,0:T(8,128)(2,1)} custom-call(bf16[16,128,256]{2,1,0:T(8,128)(2,1)} %bitcast.74), custom_call_target="tpu_custom_call" | custom-call | tf_op jit(solution)/shard_map/keys_values_back/pallas_call | solution.py:288
  220.8 1.4 reduce_sum.140
  222.2 4.0 %convolution_convert_fusion = bf16[128,4096]{1,0:T(8,128)(2,1)} fusion(bf16[4096,384]{1,0:T(8,128)(2,1)} %bitcast.68, bf16[128,256]{1,0:T(8,128)(2,1)S(1)} %reduce_sum.140, bf16[128,128]{1,0:T(8,128)(2,1)S(1)} %copy-done.15), kind=kOutput, calls=%fused_computation.1 | convolution fusion | flops 403374080 | bytes 4292608 | tf_op jit(solution)/shard_map/rc,dc->rd/dot_general | solution.py:455
  226.1 2.3 reshape.160.refs_0_
  228.5 33.1 %normed_back.1 = bf16[32,128,128]{2,1,0:T(8,128)(2,1)} custom-call(bf16[32,128,128]{2,1,0:T(8,128)(2,1)} %reshape.160.refs_0_), custom_call_target="tpu_custom_call" | custom-call | tf_op jit(solution)/shard_map/normed_back/pallas_call | solution.py:288
  261.6 1.4 convert_reduce_fusion
  263.0 0.2 multiply_reduce_fusion.3
  263.5 0.8 fusion.41.refs_0_
  264.3 14.2 %pooled_back.1 = bf16[16,128,128]{2,1,0:T(8,128)(2,1)} custom-call(bf16[128,128]{1,0:T(8,128)(2,1)} %fusion.41.refs_0_), custom_call_target="tpu_custom_call" | custom-call | tf_op jit(solution)/shard_map/pooled_back/pallas_call | solution.py:288
  278.5 2.5 fusion.2
  281.0 1.0 copy-done.4
  282.0 2.7 fusion.6
  284.7 2.5 reshape.162.refs_0_
  287.2 15.3 %dmix_sum.1 = f32[16,48,128]{2,1,0:T(8,128)} custom-call(f32[16,48,128]{2,1,0:T(8,128)} %reshape.162.refs_0_), custom_call_target="tpu_custom_call" | custom-call | tf_op jit(solution)/shard_map/dmix_sum/pallas_call | solution.py:288
  302.6 1.0 reduce_sum.145
  304.0 0.7 reshape.164.refs_0_
  304.7 12.4 %dscore_out.1 = bf16[16,48,128]{2,1,0:T(8,128)(2,1)} custom-call(bf16[48,128]{1,0:T(8,128)(2,1)} %reshape.164.refs_0_), custom_call_target="tpu_custom_call" | custom-call | tf_op jit(solution)/shard_map/dscore_out/pallas_call | solution.py:288
  317.1 1.3 reshape.165
  318.4 0.9 copy-done.9
  319.3 1.6 fusion.13.q_ref
  320.9 0.8 fusion.22
  321.8 1.7 fusion.1
  323.5 1.7 copy.60
  325.2 49.9 %tokens_back.1 = (bf16[3,64,4096]{2,1,0:T(8,128)(2,1)}, f32[32,4096]{1,0:T(8,128)}) custom-call(bf16[16,3,64,256]{3,2,1,0:T(8,128)(2,1)} %bitcast.69, f32[32,256]{1,0:T(8,128)} %fusion.13.q_ref), custom_call_target="tpu_custom_call" | custom-call | tf_op jit(solution)/shard_map/tokens_back/pallas_call | solution.py:344
  375.1 1.0 convolution_convert_fusion.8
  376.1 0.4 copy-done.12
  376.5 1.1 copy.85
  377.6 0.8 copy.86
  (77 shorter events, 1.7 us)
Async XLA Ops:
  0.6 1.0 copy-start
  82.6 3.9 %copy-start.1 = (bf16[16,3,64,256]{3,2,1,0:T(8,128)(2,1)S(1)}, bf16[16,3,64,256]{3,2,1,0:T(8,128)(2,1)}, u32[]{:S(2)}) copy-start(bf16[16,3,64,256]{3,2,1,0:T(8,128)(2,1)} %get-tuple-element.12) | copy-start | bytes 4718596
  86.5 217.3 %copy-start.2 = (f32[48,64,32]{0,2,1:T(8,128)}, f32[48,64,32]{0,2,1:T(8,128)S(1)}, u32[]{:S(2)}) copy-start(f32[48,64,32]{0,2,1:T(8,128)S(1)} %fusion.17) | copy-start | bytes 1179652
  86.5 2.0 copy-start.8
  89.2 28.3 %copy-start.14 = (f32[4096]{0:T(1024)S(1)}, f32[4096]{0:T(1024)}, u32[]{:S(2)}) copy-start(f32[4096]{0:T(1024)} %param.14) | copy-start | bytes 49156
  89.3 29.0 %copy-start.16 = (bf16[256,128]{1,0:T(8,128)(2,1)S(1)}, bf16[256,128]{1,0:T(8,128)(2,1)}, u32[]{:S(2)}) copy-start(bf16[256,128]{1,0:T(8,128)(2,1)} %param.13) | copy-start | bytes 196612
  89.3 29.0 %copy-start.17 = (bf16[256,128]{1,0:T(8,128)(2,1)S(1)}, bf16[256,128]{1,0:T(8,128)(2,1)}, u32[]{:S(2)}) copy-start(bf16[256,128]{1,0:T(8,128)(2,1)} %param.12) | copy-start | bytes 196612
  89.3 29.0 %copy-start.18 = (bf16[256,128]{1,0:T(8,128)(2,1)S(1)}, bf16[256,128]{1,0:T(8,128)(2,1)}, u32[]{:S(2)}) copy-start(bf16[256,128]{1,0:T(8,128)(2,1)} %param.11) | copy-start | bytes 196612
  115.8 0.5 copy-start.25
  116.5 35.9 %copy-start.19 = (f32[128]{0:T(128)}, f32[128]{0:T(128)S(1)}, u32[]{:S(2)}) copy-start(f32[128]{0:T(128)S(1)} %sub.79) | copy-start | bytes 1540
  116.9 0.5 copy-start.27
  117.5 34.9 %copy-start.21 = (f32[128]{0:T(128)}, f32[128]{0:T(128)S(1)}, u32[]{:S(2)}) copy-start(f32[128]{0:T(128)S(1)} %mul.118) | copy-start | bytes 1540
  157.6 23.6 %copy-start.31 = (bf16[32,4,128]{2,1,0:T(4,128)(2,1)S(1)}, bf16[32,4,128]{2,1,0:T(4,128)(2,1)}, u32[]{:S(2)}) copy-start(bf16[32,4,128]{2,1,0:T(4,128)(2,1)} %param.15) | copy-start | bytes 98308
  179.4 1.9 copy-start.10
  180.9 1.0 copy-start.6
  180.9 1.0 copy-start.23
  181.2 0.7 copy-start.29
  190.1 32.1 %copy-start.15 = (bf16[128,128]{1,0:T(8,128)(2,1)S(1)}, bf16[128,128]{1,0:T(8,128)(2,1)}, u32[]{:S(2)}) copy-start(bf16[128,128]{1,0:T(8,128)(2,1)} %copy.50) | copy-start | bytes 98308
  228.5 34.5 %copy-start.26 = (f32[4]{0:T(128)S(1)}, f32[4]{0:T(128)}, u32[]{:S(2)}) copy-start(f32[4]{0:T(128)} %copy-done.25) | copy-start | bytes 52
  228.5 34.5 %copy-start.28 = (f32[4]{0:T(128)S(1)}, f32[4]{0:T(128)}, u32[]{:S(2)}) copy-start(f32[4]{0:T(128)} %copy-done.27) | copy-start | bytes 52
  228.5 35.0 %copy-start.20 = (f32[128]{0:T(128)S(1)}, f32[128]{0:T(128)}, u32[]{:S(2)}) copy-start(f32[128]{0:T(128)} %copy-done.19) | copy-start | bytes 1540
  228.5 35.0 %copy-start.22 = (f32[128]{0:T(128)S(1)}, f32[128]{0:T(128)}, u32[]{:S(2)}) copy-start(f32[128]{0:T(128)} %copy-done.21) | copy-start | bytes 1540
  281.0 1.0 copy-start.4
  318.4 0.9 copy-start.9
  319.3 1.6 copy-start.3
  319.3 1.6 copy-start.5
  323.4 51.6 %copy-start.7 = (f32[128,2048]{1,0:T(8,128)S(1)}, f32[128,2048]{1,0:T(8,128)}, u32[]{:S(2)}) copy-start(f32[128,2048]{1,0:T(8,128)} %copy-done.6) | copy-start | bytes 3145732
  323.5 51.6 %copy-start.11 = (bf16[16,128,256]{2,1,0:T(8,128)(2,1)S(1)}, bf16[16,128,256]{2,1,0:T(8,128)(2,1)}, u32[]{:S(2)}) copy-start(bf16[16,128,256]{2,1,0:T(8,128)(2,1)} %keys_values.1) | copy-start | bytes 3145732
  323.5 51.6 %copy-start.24 = (f32[128]{0:T(128)S(1)}, f32[128]{0:T(128)}, u32[]{:S(2)}) copy-start(f32[128]{0:T(128)} %copy-done.23) | copy-start | bytes 1540
  323.5 51.6 %copy-start.30 = (f32[128]{0:T(128)S(1)}, f32[128]{0:T(128)}, u32[]{:S(2)}) copy-start(f32[128]{0:T(128)} %copy-done.29) | copy-start | bytes 1540
  375.1 1.4 copy-start.12
  376.1 1.6 copy-start.13

commit v2 on v0

v2 whole, which is shorter than its diff:
```python
import functools
from types import SimpleNamespace

import jax
import jax.numpy as jnp
from jax import lax
from jax.experimental import pallas as pl
from jax.experimental.pallas import tpu as pltpu
from jax.sharding import PartitionSpec as P

HD = 128
EPS = 1e-05
NZ = 8
MESH = pl.DeviceIdType.MESH
F32 = jnp.float32
BF16 = jnp.bfloat16
VAR, SEQ = "var", "seq"
NT = ((1,), (1,))
TN = ((0,), (0,))


def remote(src, dst, send, recv, device):
    return pltpu.make_async_remote_copy(
        src_ref=src, dst_ref=dst, send_sem=send, recv_sem=recv, device_id=device, device_id_type=MESH
    )


def loop(first, last, body):
    def step(k, carry):
        body(k)
        return carry

    lax.fori_loop(first, last, step, 0)


def slot(ref, j):
    return ref.at[j]


def dma(*shape):
    return pltpu.SemaphoreType.DMA(shape)


class Direct:
    def __init__(self, axis, n, src=slot, dst=slot):
        self.axis, self.n, self.src, self.dst = axis, n, src, dst

    def sems(self):
        return [dma(self.n), dma(self.n), dma()]

    def peers(self):
        me = lax.axis_index(self.axis)
        return [(self.n - 1, lambda k: {self.axis: lax.rem(me + k + 1, self.n)})]

    def copy(self, x, o, sems, k, received):
        me = lax.axis_index(self.axis)
        to = lax.rem(me + k, self.n)
        at = lax.rem(me + self.n - k, self.n) if received else me
        return remote(self.src(x, to), self.dst(o, at), sems[0].at[k], sems[1].at[k], {self.axis: to})

    def own(self, x, o, sems):
        me = lax.axis_index(self.axis)
        return pltpu.make_async_copy(self.src(x, me), self.dst(o, me), sems[2])

    def start(self, x, o, sems):
        self.far(x, o, sems, 0)
        self.near(x, o, sems, 0)

    def far(self, x, o, sems, near):
        loop(near + 1, self.n - near, lambda k: self.copy(x, o, sems, k, False).start())

    def near(self, x, o, sems, near):
        loop(1, near + 1, lambda k: self.copy(x, o, sems, k, False).start())
        loop(self.n - near, self.n, lambda k: self.copy(x, o, sems, k, False).start())
        self.own(x, o, sems).start()

    def landed(self, x, o, sems):
        self.own(x, o, sems).wait()
        loop(1, self.n, lambda k: self.copy(x, o, sems, k, True).wait_recv())

    def sent(self, x, o, sems):
        loop(1, self.n, lambda k: self.copy(x, o, sems, k, False).wait_send())


class GatherSeq:
    def __init__(self, n):
        self.nz = NZ
        self.nx = n // NZ

    def sems(self):
        return [dma(self.nz), dma(self.nz), dma(self.nz, self.nx), dma(self.nz, self.nx), dma()]

    def place(self):
        me = lax.axis_index(SEQ)
        return me, me // self.nz, lax.rem(me, self.nz)

    def peers(self):
        me, x, z = self.place()
        return [
            (self.nz - 1, lambda k: {SEQ: x * self.nz + lax.rem(z + k + 1, self.nz)}),
            (self.nx - 1, lambda k: {SEQ: lax.rem(x + k + 1, self.nx) * self.nz + z}),
        ]

    def along_z(self, a, o, sems, k, received):
        me, x, z = self.place()
        at = lax.rem(z + self.nz - k, self.nz) if received else z
        return remote(
            a, o.at[x * self.nz + at], sems[0].at[k], sems[1].at[k],
            {SEQ: x * self.nz + lax.rem(z + k, self.nz)},
        )

    def along_x(self, a, o, sems, k, m, received):
        me, x, z = self.place()
        zz = lax.rem(z + self.nz - k, self.nz)
        src = a if isinstance(k, int) and k == 0 else o.at[x * self.nz + zz]
        row = lax.rem(x + self.nx - m, self.nx) if received else x
        return remote(
            src, o.at[row * self.nz + zz], sems[2].at[k, m], sems[3].at[k, m],
            {SEQ: lax.rem(x + m, self.nx) * self.nz + z},
        )

    def own(self, a, o, sems):
        return pltpu.make_async_copy(a, o.at[lax.axis_index(SEQ)], sems[4])

    def start(self, a, o, sems):
        loop(1, self.nz, lambda k: self.along_z(a, o, sems, k, False).start())
        loop(1, self.nx, lambda m: self.along_x(a, o, sems, 0, m, False).start())
        self.own(a, o, sems).start()

    def middle(self, a, o, sems):
        def forward(k):
            self.along_z(a, o, sems, k, True).wait_recv()
            loop(1, self.nx, lambda m: self.along_x(a, o, sems, k, m, False).start())

        loop(1, self.nz, forward)

    def landed(self, a, o, sems):
        self.own(a, o, sems).wait()

        def wait(k):
            loop(1, self.nx, lambda m: self.along_x(a, o, sems, k, m, True).wait_recv())

        loop(0, self.nz, wait)

    def sent(self, a, o, sems):
        loop(1, self.nz, lambda k: self.along_z(a, o, sems, k, False).wait_send())

        def wait(k):
            loop(1, self.nx, lambda m: self.along_x(a, o, sems, k, m, False).wait_send())

        loop(0, self.nz, wait)


class GatherVar:
    def __init__(self, n, dst=slot):
        self.n, self.ny, self.dst = n, n // 2, dst

    def sems(self):
        return [dma(self.ny), dma(self.ny), dma(self.ny), dma(self.ny), dma()]

    def place(self):
        me = lax.axis_index(VAR)
        return me, me // 2, lax.rem(me, 2)

    def far(self, src, o, sems, block, way, k):
        me, y, c = self.place()
        at = 2 * lax.rem(y + self.ny - block, self.ny) + c
        src = self.dst(o, at) if src is None else src
        return remote(
            src, self.dst(o, at), sems[0].at[k], sems[1].at[k], {VAR: 2 * lax.rem(y + way, self.ny) + c}
        )

    def arrived(self, a, o, sems, k):
        me, y, c = self.place()
        at = 2 * lax.rem(y + self.ny - k, self.ny) + c
        remote(a, self.dst(o, at), sems[0].at[k], sems[1].at[k], {VAR: 2 * y + 1 - c}).wait_recv()

    def across(self, o, sems, k, received, first=None):
        me, y, c = self.place()
        side = 1 - c if received else c
        at = 2 * lax.rem(y + self.ny - k, self.ny) + side
        src = self.dst(o, at) if first is None else first
        return remote(src, self.dst(o, at), sems[2].at[k], sems[3].at[k], {VAR: 2 * y + 1 - c})

    def own(self, a, o, sems):
        return pltpu.make_async_copy(a, self.dst(o, lax.axis_index(VAR)), sems[4])

    def begin(self, a, o, sems):
        loop(1, self.ny, lambda k: self.far(a, o, sems, 0, k, k).start())

    def start(self, a, o, sems):
        self.begin(a, o, sems)
        self.across(o, sems, 0, False, a).start()
        self.own(a, o, sems).start()

    def middle(self, a, o, sems):
        def forward(k):
            self.arrived(a, o, sems, k)
            self.across(o, sems, k, False).start()

        loop(1, self.ny, forward)

    def landed(self, a, o, sems):
        self.own(a, o, sems).wait()
        loop(0, self.ny, lambda k: self.across(o, sems, k, True).wait_recv())

    def sent(self, a, o, sems):
        loop(1, self.ny, lambda k: self.far(a, o, sems, 0, k, k).wait_send())
        self.across(o, sems, 0, False, a).wait_send()
        loop(1, self.ny, lambda k: self.across(o, sems, k, False).wait_send())


class RingVar(GatherVar):
    def begin(self, a, o, sems):
        self.far(a, o, sems, 0, 1, 1).start()
        self.far(a, o, sems, 0, self.ny - 1, self.ny - 1).start()

    def step(self, a, o, sems, t):
        half = self.ny // 2
        self.arrived(a, o, sems, t)
        if t < half:
            self.far(None, o, sems, t, 1, t + 1).start()
        self.across(o, sems, t, False).start()
        if t < half:
            self.arrived(a, o, sems, self.ny - t)
            if t < half - 1:
                self.far(None, o, sems, self.ny - t, self.ny - 1, self.ny - t - 1).start()
            self.across(o, sems, self.ny - t, False).start()


class TwoStepVar(GatherVar):
    def begin(self, a, o, sems):
        for k in (2, 6, 1, 7):
            self.far(a, o, sems, 0, k, k).start()

    def opposite(self, o, sems):
        me, y, c = self.place()
        return self.far(None, o, sems, 2 + 4 * c, 2 + 4 * c, 4)

    def middle(self, a, o, sems):
        me, y, c = self.place()
        self.arrived(a, o, sems, 2)
        self.arrived(a, o, sems, 6)
        self.opposite(o, sems).start()
        self.far(None, o, sems, 2, 1, 3).start()
        self.far(None, o, sems, 6, 7, 5).start()
        for k in (2, 6):
            self.across(o, sems, k, False).start()
        for k in (1, 7, 3, 5, 4):
            self.arrived(a, o, sems, k)
            self.across(o, sems, k, False).start()


class ReduceVar:
    def __init__(self, n):
        self.n, self.ny = n, n // 2

    def sems(self):
        return [dma(self.ny) for _ in range(4)]

    def place(self):
        me = lax.axis_index(VAR)
        return me // 2, lax.rem(me, 2)

    def across(self, b, held, sems, k):
        y, c = self.place()
        yy = lax.rem(y + k + 1, self.ny)
        return remote(b.at[2 * yy + 1 - c], held.at[yy], sems[0].at[k], sems[1].at[k], {VAR: 2 * y + 1 - c})

    def along_y(self, summed, landed, sems, k, received):
        y, c = self.place()
        yy = lax.rem(y + k + 1, self.ny)
        at = lax.rem(y + self.ny - k - 1, self.ny) if received else y
        return remote(summed.at[yy], landed.at[at], sems[2].at[k], sems[3].at[k], {VAR: 2 * yy + c})

    def start(self, b, held, summed, landed, sems):
        loop(0, self.ny, lambda k: self.across(b, held, sems, k).start())

    def push(self, b, held, summed, landed, sems):
        y, c = self.place()

        def add(k):
            yy = lax.rem(y + k + 1, self.ny)
            self.across(b, held, sems, k).wait_recv()
            total = b[2 * yy + c].astype(F32) + held[yy].astype(F32)
            summed[yy] = total.astype(summed.dtype)

        def step(k):
            add(k)
            self.along_y(summed, landed, sems, k, False).start()

        loop(0, self.ny - 1, step)
        add(self.ny - 1)

    def landed(self, b, held, summed, landed, sems):
        y, c = self.place()
        total = summed[y].astype(F32)
        for k in range(self.ny - 1):
            self.along_y(summed, landed, sems, k, True).wait_recv()
            total = total + landed[lax.rem(y + self.ny - k - 1, self.ny)].astype(F32)
        return total

    def sent(self, b, held, summed, landed, sems):
        loop(0, self.ny, lambda k: self.across(b, held, sems, k).wait_send())
        loop(0, self.ny - 1, lambda k: self.along_y(summed, landed, sems, k, False).wait_send())


class ReduceSeq:
    def __init__(self, n):
        self.nz, self.nx = NZ, n // NZ

    def sems(self):
        return [dma(self.nz, self.nx), dma(self.nz, self.nx), dma(self.nz), dma(self.nz)]

    def place(self):
        me = lax.axis_index(SEQ)
        return me // self.nz, lax.rem(me, self.nz)

    def along_x(self, b, held, sems, k, m, received):
        x, z = self.place()
        zz = lax.rem(z + k + 1, self.nz)
        to = lax.rem(x + m, self.nx)
        row = lax.rem(x + self.nx - m, self.nx) if received else x
        return remote(
            b.at[to * self.nz + zz], held.at[row * self.nz + zz], sems[0].at[k, m], sems[1].at[k, m],
            {SEQ: to * self.nz + z},
        )

    def along_z(self, summed, landed, sems, k, received):
        x, z = self.place()
        zz = lax.rem(z + k + 1, self.nz)
        at = lax.rem(z + self.nz - k - 1, self.nz) if received else z
        return remote(summed.at[zz], landed.at[at], sems[2].at[k], sems[3].at[k], {SEQ: x * self.nz + zz})

    def start(self, b, held, summed, landed, sems):
        def send(k):
            loop(1, self.nx, lambda m: self.along_x(b, held, sems, k, m, False).start())

        loop(0, self.nz, send)

    def push(self, b, held, summed, landed, sems):
        x, z = self.place()

        def add(k):
            zz = lax.rem(z + k + 1, self.nz)
            total = b[x * self.nz + zz].astype(F32)
            for m in range(1, self.nx):
                self.along_x(b, held, sems, k, m, True).wait_recv()
                total = total + held[lax.rem(x + self.nx - m, self.nx) * self.nz + zz].astype(F32)
            summed[zz] = total.astype(summed.dtype)

        def step(k):
            add(k)
            self.along_z(summed, landed, sems, k, False).start()

        loop(0, self.nz - 1, step)
        add(self.nz - 1)

    def landed(self, b, held, summed, landed, sems):
        x, z = self.place()
        total = summed[z].astype(F32)
        for k in range(self.nz - 1):
            self.along_z(summed, landed, sems, k, True).wait_recv()
            total = total + landed[lax.rem(z + self.nz - k - 1, self.nz)].astype(F32)
        return total

    def sent(self, b, held, summed, landed, sems):
        def wait(k):
            loop(1, self.nx, lambda m: self.along_x(b, held, sems, k, m, False).wait_send())

        loop(0, self.nz, wait)
        loop(0, self.nz - 1, lambda k: self.along_z(summed, landed, sems, k, False).wait_send())


class SumAlong:
    def __init__(self, n, along_z):
        self.n, self.along_z = (NZ if along_z else n // NZ), along_z

    def sems(self):
        return [dma(self.n), dma(self.n)]

    def place(self):
        me = lax.axis_index(SEQ)
        return lax.rem(me, NZ) if self.along_z else me // NZ

    def copy(self, src, held, sems, k, received):
        me = lax.axis_index(SEQ)
        here = self.place()
        at = lax.rem(here + self.n - k, self.n) if received else here
        to = lax.rem(here + k, self.n)
        to = me // NZ * NZ + to if self.along_z else to * NZ + lax.rem(me, NZ)
        return remote(src, held.at[at], sems[0].at[k], sems[1].at[k], {SEQ: to})

    def start(self, src, held, sems):
        loop(1, self.n, lambda k: self.copy(src, held, sems, k, False).start())
        held[self.place()] = src[...]

    def landed(self, src, held, sems):
        loop(1, self.n, lambda k: self.copy(src, held, sems, k, True).wait_recv())
        total = held[0]
        for at in range(1, self.n):
            total = total + held[at]
        return total

    def sent(self, src, held, sems):
        loop(1, self.n, lambda k: self.copy(src, held, sems, k, False).wait_send())


def bound(job, sems, refs):
    def fill(phase):
        return lambda *more: phase(*refs, sems, *more)

    return SimpleNamespace(
        **{name: fill(getattr(job, name)) for name in dir(job) if not name.startswith("_") and name != "n"
           and callable(getattr(job, name))}
    )


def barrier(groups):
    sem = pltpu.get_barrier_semaphore()
    for count, to in groups:
        loop(0, count, lambda k: pl.semaphore_signal(sem, inc=1, device_id=to(k), device_id_type=MESH))
    return lambda: pl.semaphore_wait(sem, sum(count for count, _ in groups))


def dot(a, b, dims=((1,), (0,))):
    return lax.dot_general(a, b, (dims, ((), ())), preferred_element_type=F32)


def over_vars(fold, z):
    out = z[:, :128]
    for at in range(128, z.shape[1], 128):
        out = fold(out, z[:, at : at + 128])
    for shift in (64, 32, 16):
        out = fold(out, pltpu.roll(out, shift, 1))
    return jnp.concatenate([out] * (z.shape[1] // 128), axis=1)


def program(n_var, n_seq, tokens, agg_query, agg_value, w_query, w_key, w_value, gain, grad_out):
    factor = HD ** (-0.5)
    per, rows, width = tokens.shape
    heads = agg_query.shape[0]
    octets = heads // 8
    cut = width // n_var
    own = rows // n_var
    line = own * heads
    groups = rows // 16
    chunk = per * 16
    lanes = n_var * chunk
    tall = 16 * heads
    row_count = n_seq * own
    at_once = 16 // own
    ny, nz, nx = n_var // 2, NZ, n_seq // NZ

    at_cut = lambda j: pl.ds(pl.multiple_of(j * cut, cut), cut)
    weight = lambda w: RingVar(n_var, lambda o, j: o.at[j, :, pl.ds(w * HD, HD)])
    jobs = dict(
        tokens=Direct(VAR, n_var, lambda x, j: x.at[:, :, at_cut(j)], slot),
        scores=GatherVar(n_var),
        value=GatherSeq(n_seq),
        pooled=ReduceVar(n_var),
        normed=GatherSeq(n_seq),
        w_query=weight(0),
        w_key=weight(1),
        w_value=weight(2),
        kv=TwoStepVar(n_var),
        dkv=ReduceVar(n_var),
        grad=ReduceSeq(n_seq),
        d_pooled=GatherVar(n_var),
        dmix=ReduceVar(n_var),
        dscore=GatherVar(n_var),
        back=Direct(VAR, n_var, slot, lambda o, j: o.at[:, :, at_cut(j)]),
        query_z=SumAlong(n_seq, True),
        query_x=SumAlong(n_seq, False),
        query=GatherVar(n_var, lambda o, j: o.at[:, at_cut(j)]),
    )

    block = lambda n, r=line, c=HD, t=BF16: ((n, r, c), t)

    def through(blocks, *rest):
        return block(blocks, *rest), block(ny, *rest), block(ny, *rest), block(ny, *rest)

    pooled, dkv = through(n_var), through(n_var, row_count, 2 * HD)
    dmix = through(n_var, 8, lanes, F32)
    buffers = dict(
        grouped=((n_var, per, rows, cut), BF16),
        s_own=((heads, 256), F32),
        s_all=block(n_var, heads, 256, F32),
        value_all=block(n_seq, cut, HD),
        mix=block(n_var, 8, lanes, F32),
        mix_wide=block(groups, tall, lanes),
        mix_tall=block(groups, lanes, tall),
        summary=block(groups, tall, cut),
        stack=block(groups, tall, HD),
        pooled0=pooled[0], pooled1=pooled[1], pooled2=pooled[2], pooled3=pooled[3],
        unit=((line, HD), F32),
        inv=((line, HD), F32),
        normed_own=((line, HD), BF16),
        normed_all=block(n_seq),
        weights=block(n_var, cut, 3 * HD),
        wide=((row_count, width), BF16),
        kv_own=((row_count, 2 * HD), BF16),
        kv_all=block(n_var, row_count, 2 * HD),
        dkv0=dkv[0], dkv1=dkv[1], dkv2=dkv[2], dkv3=dkv[3],
        grad0=block(n_seq), grad1=block(n_seq), grad2=block(nz), grad3=block(nz),
        dp_own=((line, HD), BF16),
        dp_all=block(n_var),
        d_summary=block(groups, tall, cut),
        dmix0=dmix[0], dmix1=dmix[1], dmix2=dmix[2], dmix3=dmix[3],
        dscore_own=((8, lanes), F32),
        dscore_all=block(n_var, 8, lanes, F32),
        back_b=((n_var, per, rows, cut), BF16),
        query_part=((heads, cut), F32),
        query_line=((heads, cut), F32),
        query_done=((heads, cut), F32),
        query_z=block(nz, heads, cut, F32),
        query_x=block(nx, heads, cut, F32),
    )
    results = dict(
        attended=((row_count, HD), BF16),
        mixed=(tokens.shape, BF16),
        dscore=((heads, per * rows), BF16),
        d_query=((heads, width), F32),
    )
    names = [*results, *buffers]
    job_sems = [job.sems() for job in jobs.values()]

    def kernel(tok, aq, av, wq, wk, wv, gn, go, *rest):
        r = SimpleNamespace(**dict(zip(names, rest)))
        refs = dict(
            tokens=(tok, r.grouped),
            scores=(r.s_own, r.s_all),
            value=(av, r.value_all),
            pooled=(r.pooled0, r.pooled1, r.pooled2, r.pooled3),
            normed=(r.normed_own, r.normed_all),
            w_query=(wq, r.weights),
            w_key=(wk, r.weights),
            w_value=(wv, r.weights),
            kv=(r.kv_own, r.kv_all),
            dkv=(r.dkv0, r.dkv1, r.dkv2, r.dkv3),
            grad=(r.grad0, r.grad1, r.grad2, r.grad3),
            d_pooled=(r.dp_own, r.dp_all),
            dmix=(r.dmix0, r.dmix1, r.dmix2, r.dmix3),
            dscore=(r.dscore_own, r.dscore_all),
            back=(r.back_b, r.mixed),
            query_z=(r.query_part, r.query_z),
            query_x=(r.query_line, r.query_x),
            query=(r.query_done, r.d_query),
        )
        left, ready_jobs = list(rest[len(names) :]), {}
        for (name, job), wanted in zip(jobs.items(), job_sems):
            ready_jobs[name] = bound(job, left[: len(wanted)], refs[name])
            left = left[len(wanted) :]
        j = SimpleNamespace(**ready_jobs)
        ring = (j.w_key, j.w_value, j.w_query)

        def t_group(g):
            return r.grouped[:, :, g * 16 : (g + 1) * 16, :].reshape(lanes, cut)

        i = lax.axis_index(VAR)
        greeted = barrier(jobs["tokens"].peers() + jobs["value"].peers())

        rows_here = [tok[v, g * 16 : (g + 1) * 16, :] for g in range(groups) for v in range(per)]
        local = dot(aq[...], jnp.concatenate(rows_here, axis=0), NT) * factor
        r.s_own[...] = jnp.concatenate([local, jnp.zeros((heads, 256 - per * rows), F32)], axis=1)
        greeted()
        j.scores.start()
        j.value.start()
        j.tokens.start()
        j.scores.middle()
        j.value.middle()

        iota = lambda shape, dim: lax.broadcasted_iota(jnp.int32, shape, dim)
        ones = lambda where: where.astype(F32).astype(BF16)
        wide_mask = lax.rem(iota((16, lanes), 1), 16) == iota((16, lanes), 0)
        tall_mask = lax.rem(iota((lanes, tall), 0), 16) == lax.rem(iota((lanes, tall), 1), 16)
        spread_heads = ones(iota((heads, tall), 1) // 16 == iota((heads, tall), 0))
        at, to = iota((tall, tall), 0), iota((tall, tall), 1)
        to_patches = ones(to == lax.rem(at, heads) * 16 + at // heads)
        to_heads = ones(to == lax.rem(at, 16) * heads + at // 16)

        j.scores.landed()
        for g in range(groups):
            z = jnp.concatenate([r.s_all[n, :, g * chunk : (g + 1) * chunk] for n in range(n_var)], axis=1)
            e = jnp.exp(z - over_vars(jnp.maximum, z))
            mixw = e / over_vars(jnp.add, e)
            for o in range(octets):
                r.mix[g * octets + o] = mixw[o * 8 : (o + 1) * 8]
            mix_b = mixw.astype(BF16)
            full = jnp.broadcast_to(mix_b.astype(F32)[:, None, :], (heads, 16, lanes))
            full = jnp.where(wide_mask[None], full, 0.0)
            r.mix_wide[g] = full.astype(BF16).reshape(tall, lanes)
            r.mix_tall[g] = jnp.where(tall_mask, dot(mix_b, spread_heads, TN), 0.0).astype(BF16)
        j.value.landed()
        j.scores.sent()
        j.value.sent()
        j.tokens.landed()
        for w in ring:
            w.start()

        for g in range(groups):
            r.summary[g] = dot(r.mix_wide[g], t_group(g)).astype(BF16)
        for h in range(heads):
            here = slice(h * 16, (h + 1) * 16)
            part = jnp.concatenate([r.summary[g, here, :] for g in range(groups)], axis=0)
            part = dot(part, r.value_all[h]).astype(BF16)
            for g in range(groups):
                r.stack[g, here, :] = part[g * 16 : (g + 1) * 16]
        for g in range(groups):
            part = dot(to_patches, r.stack[g]).astype(BF16)
            for n in range(at_once):
                r.pooled0[g * at_once + n] = part[n * line : (n + 1) * line]
        j.pooled.start()
        j.pooled.push()
        for w in ring:
            w.step(1)
        pooled = j.pooled.landed().astype(BF16).astype(F32).reshape(own, heads, HD)
        mean = lambda a: jnp.sum(jnp.sum(a, axis=1, keepdims=True), axis=2, keepdims=True) / width
        center = mean(pooled)
        inv_std = lax.rsqrt(mean((pooled - center) ** 2) + EPS)
        unit = (pooled - center) * inv_std
        r.normed_own[...] = (unit * gn[...][None]).astype(BF16).reshape(line, HD)
        j.normed.start()
        r.unit[...] = unit.reshape(line, HD)
        r.inv[...] = jnp.broadcast_to(inv_std, (own, heads, HD)).reshape(line, HD)
        for w in ring:
            w.step(2)
        j.normed.middle()
        for t in range(3, ny // 2 + 1):
            for w in ring:
                w.step(t)
        j.normed.landed()

        def widen(g):
            src = r.normed_all[pl.ds(g * at_once, at_once)].reshape(tall, HD)
            part = dot(to_heads, src).astype(BF16)
            for h in range(heads):
                r.wide[pl.ds(pl.multiple_of(g * 16, 16), 16), h * HD : (h + 1) * HD] = part[h * 16 : (h + 1) * 16]

        loop(0, n_seq // at_once, widen)
        j.w_key.landed()
        j.w_value.landed()
        kv_weights = r.weights[:, :, HD:].reshape(width, 2 * HD)
        r.kv_own[...] = dot(r.wide[...], kv_weights).astype(BF16)
        j.kv.start()
        j.w_query.landed()
        queries = dot(r.wide[...], r.weights[:, :, :HD].reshape(width, HD)).astype(BF16)
        j.kv.middle()
        j.kv.landed()

        keys = r.kv_all[:, :, :HD].reshape(n_var * row_count, HD)
        values = r.kv_all[:, :, HD:].reshape(n_var * row_count, HD)
        grad = go[...]
        logits = dot(queries, keys, NT) * factor
        expo = jnp.exp(logits - jnp.max(logits, axis=1, keepdims=True))
        probs = expo / jnp.sum(expo, axis=1, keepdims=True)
        probs_b = probs.astype(BF16)
        dprob = dot(grad, values, NT)
        dlogit = (probs * (dprob - jnp.sum(probs * dprob, axis=1, keepdims=True)) * factor).astype(BF16)
        r.dkv0[:, :, :HD] = dot(dlogit, queries, TN).astype(BF16).reshape(n_var, row_count, HD)
        r.dkv0[:, :, HD:] = dot(probs_b, grad, TN).astype(BF16).reshape(n_var, row_count, HD)
        j.dkv.start()
        r.attended[...] = dot(probs_b, values).astype(BF16)
        dquery = dot(dlogit, keys).astype(BF16)
        j.dkv.push()
        dkv = j.dkv.landed().astype(BF16)

        dqkv = jnp.concatenate([dquery, dkv], axis=1)
        r.wide[...] = dot(dqkv, r.weights[...].reshape(width, 3 * HD), NT).astype(BF16)

        def narrow(g):
            at = pl.ds(pl.multiple_of(g * 16, 16), 16)
            src = jnp.concatenate([r.wide[at, h * HD : (h + 1) * HD] for h in range(heads)], axis=0)
            part = dot(to_patches, src).astype(BF16)
            for n in range(at_once):
                r.grad0[g * at_once + n] = part[n * line : (n + 1) * line]

        loop(0, n_seq // at_once, narrow)
        j.grad.start()
        j.grad.push()
        scaled = j.grad.landed().reshape(own, heads, HD) * gn[...][None]
        unit = r.unit[...].reshape(own, heads, HD)
        inv_std = r.inv[...].reshape(own, heads, HD)
        d_pooled = inv_std * (scaled - mean(scaled) - unit * mean(scaled * unit))
        r.dp_own[...] = d_pooled.astype(BF16).reshape(line, HD)
        j.d_pooled.start()
        j.d_pooled.middle()
        j.d_pooled.landed()

        for g in range(groups):
            src = r.dp_all[g * at_once : (g + 1) * at_once].reshape(tall, HD)
            r.stack[g] = dot(to_heads, src).astype(BF16)
        for h in range(heads):
            here = slice(h * 16, (h + 1) * 16)
            part = jnp.concatenate([r.stack[g, here, :] for g in range(groups)], axis=0)
            part = dot(part, r.value_all[h], NT).astype(BF16)
            for g in range(groups):
                r.d_summary[g, here, :] = part[g * 16 : (g + 1) * 16]
        for g in range(groups):
            cross = dot(r.d_summary[g], t_group(g), NT).reshape(heads, 16, lanes)
            dmix = jnp.sum(jnp.where(wide_mask[None], cross, 0.0), axis=1)
            for o in range(octets):
                r.dmix0[g * octets + o] = dmix[o * 8 : (o + 1) * 8]
        j.dmix.start()
        for g in range(groups):
            part = dot(r.mix_tall[g], r.d_summary[g]).astype(BF16)
            r.back_b[:, :, g * 16 : (g + 1) * 16, :] = part.reshape(n_var, per, 16, cut)
        j.dmix.push()
        j.back.far(4)
        dmix = j.dmix.landed()
        mixw = r.mix[i]
        dscore = mixw * (dmix - over_vars(jnp.add, mixw * dmix)) * factor
        r.dscore_own[...] = dscore.astype(BF16).astype(F32)
        j.dscore.start()
        j.back.near(4)
        j.dscore.middle()
        j.dscore.landed()

        query_part = jnp.zeros((heads, cut), F32)
        mine = jnp.zeros((heads, per * rows), F32)
        lane, column = iota((lanes, per * rows), 0) - i * chunk, iota((lanes, per * rows), 1)
        for g in range(groups):
            dscore = r.dscore_all[g * octets : (g + 1) * octets].reshape(heads, lanes).astype(BF16)
            query_part = query_part + dot(dscore, t_group(g))
            at_lane = column // rows * 16 + lax.rem(column, 16)
            here = (lane == at_lane) & (lax.rem(column, rows) // 16 == g)
            mine = mine + dot(dscore, ones(here))
        r.query_part[...] = query_part
        j.query_z.start()
        r.dscore[...] = mine.astype(BF16)
        r.query_line[...] = j.query_z.landed()
        j.query_x.start()
        r.query_done[...] = j.query_x.landed()
        j.query.start()
        j.query.middle()
        for job in (j.tokens, j.pooled, j.normed, *ring, j.kv, j.dkv, j.grad, j.d_pooled, j.dmix, j.dscore):
            job.sent()
        j.query_z.sent()
        j.query_x.sent()
        j.query.landed()
        j.query.sent()
        j.back.landed()
        j.back.sent()

    in_vmem = pl.BlockSpec(memory_space=pltpu.VMEM)
    return pl.pallas_call(
        kernel,
        name="encoder",
        out_shape=[jax.ShapeDtypeStruct(*results[name]) for name in results],
        in_specs=[in_vmem] * 8,
        out_specs=[in_vmem] * len(results),
        scratch_shapes=[pltpu.VMEM(*buffers[name]) for name in buffers]
        + [sem for wanted in job_sems for sem in wanted],
        compiler_params=pltpu.CompilerParams(
            collective_id=0, has_side_effects=True, vmem_limit_bytes=60 * 1024 * 1024
        ),
    )(tokens, agg_query, agg_value, w_query, w_key, w_value, gain, grad_out)


def per_device(n_var, n_seq, tokens, agg_query, agg_value, w_query, w_key, w_value, gain, d_out):
    heads = agg_query.shape[0]
    attended, mixed, dscore, d_query = program(
        n_var, n_seq, tokens, agg_query, agg_value, w_query, w_key, w_value,
        gain.reshape(heads, HD), d_out.reshape(-1, HD),
    )
    through_scores = dot(dscore, agg_query, TN).reshape(tokens.shape)
    d_tokens = (mixed.astype(F32) + through_scores).astype(BF16)
    return (attended.reshape(d_out.shape), d_tokens, d_query)


def solution(mesh):
    return jax.shard_map(
        functools.partial(per_device, mesh.shape[VAR], mesh.shape[SEQ]),
        mesh=mesh,
        in_specs=(
            P(VAR, SEQ, None),
            P(),
            P(VAR, SEQ),
            P(VAR, SEQ),
            P(VAR, SEQ),
            P(VAR, SEQ),
            P(),
            P(None, VAR, SEQ),
        ),
        out_specs=(P(None, VAR, SEQ), P(VAR, SEQ, None), P()),
        check_vma=False,
    )
```

time: 1050 us -> 223 us (0.21)
  waiting for transfers between devices: 740 us -> 0 us
  Pallas kernels: 0 us -> 217 us
  blocking collectives: 174 us -> 0 us
  starting transfers between devices: 42.4 us -> 0 us
  matrix products: 36.8 us -> 1.67 us
  local copies, waits for them, and re-layouts: 22.5 us -> 1.42 us
  other arithmetic: 16.7 us -> 1.51 us
  between operations: 14.2 us -> 0.68 us
    psum x2 -> x0, waiting for transfers between devices: 393 us -> none  [the longest x1 237 us: per_device(): d_query = lax.psum(query_part, ('var', 'seq'))]
    pallas_call x0 -> x1, Pallas kernels: none -> 217 us  [program(): pl.pallas_call(kernel, name='encoder', out_shape=[jax.ShapeDtypeStruct(*r...]
    all_gather x5 -> x0, waiting for transfers between devices: 172 us -> none  [the longest x1 71 us: per_device(): lax.all_gather(pooled, 'seq', axis=1, tiled=True).astype(jnp.float32)]
    reduce_scatter x2 -> x0, waiting for transfers between devices: 110 us -> none  [the longest x1 57.9 us: per_device(): lax.psum_scatter(dvals[0].astype(jnp.bfloat16), 'var', scatter_dimension=...]
    all_to_all x2 -> x0, blocking collectives: 80.5 us -> none  [the longest x1 60.4 us: per_device(): lax.all_to_all(tokens, 'var', split_axis=1, concat_axis=0, tiled=True)]
    all_to_all x2 -> x0, waiting for transfers between devices: 62.2 us -> none  [the longest x1 34.9 us: per_device(): lax.all_to_all(grad_tok.astype(jnp.bfloat16), 'var', split_axis=0, concat...]
    psum x1 -> x0, blocking collectives: 58.5 us -> none  [per_device(): full_unit_dot = lax.psum(share_dot, 'seq')]
    all_to_all x2 -> x0, starting transfers between devices: 42 us -> none  [the longest x1 30.1 us: per_device(): lax.all_to_all(grad_tok.astype(jnp.bfloat16), 'var', split_axis=0, concat...]
  transfers between devices with their start and end apart: 11 -> 0, of which waited for: 11 -> 0; matrix products, arithmetic and copies ran while one was open for 2% -> 0% of each run, Pallas kernels for 0% -> 0%
where the time goes in v2:
time: 223 us
  Pallas kernels  217 us (97%)
    pallas_call x1, Pallas kernels, program(): pl.pallas_call(kernel, name='encoder', out_shape=[jax.ShapeDtypeStruct(*r...  217 us

profile of v2, /device:TPU:1, one launch (start us, length us, event | category | flops | bytes accessed | tf_op | source)
XLA Modules:
  0.0 222.6 jit_solution(13824156018232871482)
XLA Ops:
  0.6 217.4 %encoder.1 = (bf16[128,128]{1,0:T(8,128)(2,1)}, bf16[3,64,4096]{2,1,0:T(8,128)(2,1)}, bf16[32,192]{1,0:T(8,128)(2,1)}, f32[32,4096]{1,0:T(8,128)}) custom-call(bf16[3,64,4096]{2,1,0:T(8,128)(2,1)} %tok.1, bf16[32,4096]{1,0:T(8,128)(2,1)} %aq.1, bf16[256,128]{1,0:T(8,128)(2,1)} %av.1, bf16[256,128]{1,0:T(8,128)(2,1)} %wq.1, bf16[256,128]{1,0:T(8,128)(2,1)} %wk.1, ...), custom_call_target="tpu_custom_call" | custom-call | tf_op jit(solution)/shard_map/encoder/pallas_call | solution.py:746
  218.0 0.0 copy-start
  218.0 1.7 fusion
  219.7 0.0 copy-done
  219.7 0.0 copy-start.2
  219.7 0.0 copy-start.1
  219.7 1.5 add_convert_fusion
  221.2 0.0 copy-done.2
  221.2 0.6 copy.13
  221.9 0.0 copy-done.1
  221.9 0.8 copy.14
Async XLA Ops:
  218.0 1.7 copy-start
  219.7 1.5 copy-start.2
  219.7 2.1 copy-start.1

commit v3 on v2

--- a/solution.py
+++ b/solution.py
@@ -41,45 +41,57 @@
     return pltpu.SemaphoreType.DMA(shape)
 
 
+def first_blocks(ref, n):
+    return ref.at[pl.ds(0, n)]
+
+
+def arrived(ref, sem):
+    remote(ref, ref, sem, sem, {}).wait_recv()
+
+
+def left(ref, sem):
+    remote(ref, ref, sem, sem, {}).wait_send()
+
+
 class Direct:
-    def __init__(self, axis, n, src=slot, dst=slot):
-        self.axis, self.n, self.src, self.dst = axis, n, src, dst
+    def __init__(self, axis, n, src=slot, dst=slot, blocks=first_blocks):
+        self.axis, self.n, self.src, self.dst, self.blocks = axis, n, src, dst, blocks
 
     def sems(self):
-        return [dma(self.n), dma(self.n), dma()]
+        return [dma(), dma(), dma()]
 
     def peers(self):
         me = lax.axis_index(self.axis)
         return [(self.n - 1, lambda k: {self.axis: lax.rem(me + k + 1, self.n)})]
 
-    def copy(self, x, o, sems, k, received):
+    def send(self, x, o, sems, k):
         me = lax.axis_index(self.axis)
         to = lax.rem(me + k, self.n)
-        at = lax.rem(me + self.n - k, self.n) if received else me
-        return remote(self.src(x, to), self.dst(o, at), sems[0].at[k], sems[1].at[k], {self.axis: to})
+        remote(self.src(x, to), self.dst(o, me), sems[0], sems[1], {self.axis: to}).start()
 
     def own(self, x, o, sems):
         me = lax.axis_index(self.axis)
         return pltpu.make_async_copy(self.src(x, me), self.dst(o, me), sems[2])
 
     def start(self, x, o, sems):
-        self.far(x, o, sems, 0)
-        self.near(x, o, sems, 0)
-
-    def far(self, x, o, sems, near):
-        loop(near + 1, self.n - near, lambda k: self.copy(x, o, sems, k, False).start())
-
-    def near(self, x, o, sems, near):
-        loop(1, near + 1, lambda k: self.copy(x, o, sems, k, False).start())
-        loop(self.n - near, self.n, lambda k: self.copy(x, o, sems, k, False).start())
+        loop(1, self.n, lambda k: self.send(x, o, sems, k))
         self.own(x, o, sems).start()
+
+    def some(self, x, o, sems, *offsets):
+        for k in offsets:
+            if k == 0:
+                self.own(x, o, sems).start()
+            else:
+                self.send(x, o, sems, k)
+                if 2 * k != self.n:
+                    self.send(x, o, sems, self.n - k)
 
     def landed(self, x, o, sems):
         self.own(x, o, sems).wait()
-        loop(1, self.n, lambda k: self.copy(x, o, sems, k, True).wait_recv())
+        arrived(self.blocks(o, self.n - 1), sems[1])
 
     def sent(self, x, o, sems):
-        loop(1, self.n, lambda k: self.copy(x, o, sems, k, False).wait_send())
+        left(self.blocks(o, self.n - 1), sems[0])
 
 
 class GatherSeq:
@@ -88,7 +100,7 @@
         self.nx = n // NZ
 
     def sems(self):
-        return [dma(self.nz), dma(self.nz), dma(self.nz, self.nx), dma(self.nz, self.nx), dma()]
+        return [dma(), dma(self.nz), dma(), dma(self.nx), dma()]
 
     def place(self):
         me = lax.axis_index(SEQ)
@@ -105,58 +117,47 @@
         me, x, z = self.place()
         at = lax.rem(z + self.nz - k, self.nz) if received else z
         return remote(
-            a, o.at[x * self.nz + at], sems[0].at[k], sems[1].at[k],
+            a, o.at[x * self.nz + at], sems[0], sems[1].at[k],
             {SEQ: x * self.nz + lax.rem(z + k, self.nz)},
         )
 
-    def along_x(self, a, o, sems, k, m, received):
+    def along_x(self, a, o, sems, k, m):
         me, x, z = self.place()
-        zz = lax.rem(z + self.nz - k, self.nz)
-        src = a if isinstance(k, int) and k == 0 else o.at[x * self.nz + zz]
-        row = lax.rem(x + self.nx - m, self.nx) if received else x
-        return remote(
-            src, o.at[row * self.nz + zz], sems[2].at[k, m], sems[3].at[k, m],
-            {SEQ: lax.rem(x + m, self.nx) * self.nz + z},
-        )
+        at = x * self.nz + lax.rem(z + self.nz - k, self.nz)
+        src = a if isinstance(k, int) and k == 0 else o.at[at]
+        to = lax.rem(x + m, self.nx) * self.nz + z
+        remote(src, o.at[at], sems[2], sems[3].at[m], {SEQ: to}).start()
 
     def own(self, a, o, sems):
         return pltpu.make_async_copy(a, o.at[lax.axis_index(SEQ)], sems[4])
 
     def start(self, a, o, sems):
         loop(1, self.nz, lambda k: self.along_z(a, o, sems, k, False).start())
-        loop(1, self.nx, lambda m: self.along_x(a, o, sems, 0, m, False).start())
+        loop(1, self.nx, lambda m: self.along_x(a, o, sems, 0, m))
         self.own(a, o, sems).start()
 
     def middle(self, a, o, sems):
         def forward(k):
             self.along_z(a, o, sems, k, True).wait_recv()
-            loop(1, self.nx, lambda m: self.along_x(a, o, sems, k, m, False).start())
+            loop(1, self.nx, lambda m: self.along_x(a, o, sems, k, m))
 
         loop(1, self.nz, forward)
 
     def landed(self, a, o, sems):
         self.own(a, o, sems).wait()
-
-        def wait(k):
-            loop(1, self.nx, lambda m: self.along_x(a, o, sems, k, m, True).wait_recv())
-
-        loop(0, self.nz, wait)
+        loop(1, self.nx, lambda m: arrived(first_blocks(o, self.nz), sems[3].at[m]))
 
     def sent(self, a, o, sems):
-        loop(1, self.nz, lambda k: self.along_z(a, o, sems, k, False).wait_send())
-
-        def wait(k):
-            loop(1, self.nx, lambda m: self.along_x(a, o, sems, k, m, False).wait_send())
-
-        loop(0, self.nz, wait)
+        left(first_blocks(o, self.nz - 1), sems[0])
+        left(first_blocks(o, self.nz * (self.nx - 1)), sems[2])
 
 
 class GatherVar:
-    def __init__(self, n, dst=slot):
-        self.n, self.ny, self.dst = n, n // 2, dst
+    def __init__(self, n, dst=slot, blocks=first_blocks):
+        self.n, self.ny, self.dst, self.blocks = n, n // 2, dst, blocks
 
     def sems(self):
-        return [dma(self.ny), dma(self.ny), dma(self.ny), dma(self.ny), dma()]
+        return [dma(), dma(self.ny), dma(), dma(), dma()]
 
     def place(self):
         me = lax.axis_index(VAR)
@@ -167,20 +168,17 @@
         at = 2 * lax.rem(y + self.ny - block, self.ny) + c
         src = self.dst(o, at) if src is None else src
         return remote(
-            src, self.dst(o, at), sems[0].at[k], sems[1].at[k], {VAR: 2 * lax.rem(y + way, self.ny) + c}
+            src, self.dst(o, at), sems[0], sems[1].at[k], {VAR: 2 * lax.rem(y + way, self.ny) + c}
         )
 
     def arrived(self, a, o, sems, k):
         me, y, c = self.place()
-        at = 2 * lax.rem(y + self.ny - k, self.ny) + c
-        remote(a, self.dst(o, at), sems[0].at[k], sems[1].at[k], {VAR: 2 * y + 1 - c}).wait_recv()
-
-    def across(self, o, sems, k, received, first=None):
+        arrived(self.dst(o, 2 * lax.rem(y + self.ny - k, self.ny) + c), sems[1].at[k])
+
+    def across(self, o, sems, k, first=None):
         me, y, c = self.place()
-        side = 1 - c if received else c
-        at = 2 * lax.rem(y + self.ny - k, self.ny) + side
-        src = self.dst(o, at) if first is None else first
-        return remote(src, self.dst(o, at), sems[2].at[k], sems[3].at[k], {VAR: 2 * y + 1 - c})
+        at = self.dst(o, 2 * lax.rem(y + self.ny - k, self.ny) + c)
+        remote(at if first is None else first, at, sems[2], sems[3], {VAR: 2 * y + 1 - c}).start()
 
     def own(self, a, o, sems):
         return pltpu.make_async_copy(a, self.dst(o, lax.axis_index(VAR)), sems[4])
@@ -190,24 +188,23 @@
 
     def start(self, a, o, sems):
         self.begin(a, o, sems)
-        self.across(o, sems, 0, False, a).start()
+        self.across(o, sems, 0, a)
         self.own(a, o, sems).start()
 
     def middle(self, a, o, sems):
         def forward(k):
             self.arrived(a, o, sems, k)
-            self.across(o, sems, k, False).start()
+            self.across(o, sems, k)
 
         loop(1, self.ny, forward)
 
     def landed(self, a, o, sems):
         self.own(a, o, sems).wait()
-        loop(0, self.ny, lambda k: self.across(o, sems, k, True).wait_recv())
+        arrived(self.blocks(o, self.ny), sems[3])
 
     def sent(self, a, o, sems):
-        loop(1, self.ny, lambda k: self.far(a, o, sems, 0, k, k).wait_send())
-        self.across(o, sems, 0, False, a).wait_send()
-        loop(1, self.ny, lambda k: self.across(o, sems, k, False).wait_send())
+        left(self.blocks(o, self.ny - 1), sems[0])
+        left(self.blocks(o, self.ny), sems[2])
 
 
 class RingVar(GatherVar):
@@ -220,12 +217,12 @@
         self.arrived(a, o, sems, t)
         if t < half:
             self.far(None, o, sems, t, 1, t + 1).start()
-        self.across(o, sems, t, False).start()
+        self.across(o, sems, t)
         if t < half:
             self.arrived(a, o, sems, self.ny - t)
             if t < half - 1:
                 self.far(None, o, sems, self.ny - t, self.ny - 1, self.ny - t - 1).start()
-            self.across(o, sems, self.ny - t, False).start()
+            self.across(o, sems, self.ny - t)
 
 
 class TwoStepVar(GatherVar):
@@ -245,10 +242,10 @@
         self.far(None, o, sems, 2, 1, 3).start()
         self.far(None, o, sems, 6, 7, 5).start()
         for k in (2, 6):
-            self.across(o, sems, k, False).start()
+            self.across(o, sems, k)
         for k in (1, 7, 3, 5, 4):
             self.arrived(a, o, sems, k)
-            self.across(o, sems, k, False).start()
+            self.across(o, sems, k)
 
 
 class ReduceVar:
@@ -256,7 +253,7 @@
         self.n, self.ny = n, n // 2
 
     def sems(self):
-        return [dma(self.ny) for _ in range(4)]
+        return [dma(), dma(self.ny), dma(), dma()]
 
     def place(self):
         me = lax.axis_index(VAR)
@@ -265,13 +262,12 @@
     def across(self, b, held, sems, k):
         y, c = self.place()
         yy = lax.rem(y + k + 1, self.ny)
-        return remote(b.at[2 * yy + 1 - c], held.at[yy], sems[0].at[k], sems[1].at[k], {VAR: 2 * y + 1 - c})
-
-    def along_y(self, summed, landed, sems, k, received):
+        return remote(b.at[2 * yy + 1 - c], held.at[yy], sems[0], sems[1].at[k], {VAR: 2 * y + 1 - c})
+
+    def along_y(self, summed, landed, sems, k):
         y, c = self.place()
         yy = lax.rem(y + k + 1, self.ny)
-        at = lax.rem(y + self.ny - k - 1, self.ny) if received else y
-        return remote(summed.at[yy], landed.at[at], sems[2].at[k], sems[3].at[k], {VAR: 2 * yy + c})
+        remote(summed.at[yy], landed.at[y], sems[2], sems[3], {VAR: 2 * yy + c}).start()
 
     def start(self, b, held, summed, landed, sems):
         loop(0, self.ny, lambda k: self.across(b, held, sems, k).start())
@@ -287,7 +283,7 @@
 
         def step(k):
             add(k)
-            self.along_y(summed, landed, sems, k, False).start()
+            self.along_y(summed, landed, sems, k)
 
         loop(0, self.ny - 1, step)
         add(self.ny - 1)
@@ -295,14 +291,14 @@
     def landed(self, b, held, summed, landed, sems):
         y, c = self.place()
         total = summed[y].astype(F32)
+        arrived(first_blocks(landed, self.ny - 1), sems[3])
         for k in range(self.ny - 1):
-            self.along_y(summed, landed, sems, k, True).wait_recv()
             total = total + landed[lax.rem(y + self.ny - k - 1, self.ny)].astype(F32)
         return total
 
     def sent(self, b, held, summed, landed, sems):
-        loop(0, self.ny, lambda k: self.across(b, held, sems, k).wait_send())
-        loop(0, self.ny - 1, lambda k: self.along_y(summed, landed, sems, k, False).wait_send())
+        left(first_blocks(b, self.ny), sems[0])
+        left(first_blocks(landed, self.ny - 1), sems[2])
 
 
 class ReduceSeq:
@@ -310,31 +306,28 @@
         self.nz, self.nx = NZ, n // NZ
 
     def sems(self):
-        return [dma(self.nz, self.nx), dma(self.nz, self.nx), dma(self.nz), dma(self.nz)]
+        return [dma(), dma(self.nz), dma(), dma()]
 
     def place(self):
         me = lax.axis_index(SEQ)
         return me // self.nz, lax.rem(me, self.nz)
 
-    def along_x(self, b, held, sems, k, m, received):
+    def along_x(self, b, held, sems, k, m):
         x, z = self.place()
         zz = lax.rem(z + k + 1, self.nz)
         to = lax.rem(x + m, self.nx)
-        row = lax.rem(x + self.nx - m, self.nx) if received else x
-        return remote(
-            b.at[to * self.nz + zz], held.at[row * self.nz + zz], sems[0].at[k, m], sems[1].at[k, m],
-            {SEQ: to * self.nz + z},
-        )
-
-    def along_z(self, summed, landed, sems, k, received):
+        remote(
+            b.at[to * self.nz + zz], held.at[x * self.nz + zz], sems[0], sems[1].at[k], {SEQ: to * self.nz + z}
+        ).start()
+
+    def along_z(self, summed, landed, sems, k):
         x, z = self.place()
         zz = lax.rem(z + k + 1, self.nz)
-        at = lax.rem(z + self.nz - k - 1, self.nz) if received else z
-        return remote(summed.at[zz], landed.at[at], sems[2].at[k], sems[3].at[k], {SEQ: x * self.nz + zz})
+        remote(summed.at[zz], landed.at[z], sems[2], sems[3], {SEQ: x * self.nz + zz}).start()
 
     def start(self, b, held, summed, landed, sems):
         def send(k):
-            loop(1, self.nx, lambda m: self.along_x(b, held, sems, k, m, False).start())
+            loop(1, self.nx, lambda m: self.along_x(b, held, sems, k, m))
 
         loop(0, self.nz, send)
 
@@ -344,14 +337,14 @@
         def add(k):
             zz = lax.rem(z + k + 1, self.nz)
             total = b[x * self.nz + zz].astype(F32)
+            arrived(first_blocks(held, self.nx - 1), sems[1].at[k])
             for m in range(1, self.nx):
-                self.along_x(b, held, sems, k, m, True).wait_recv()
                 total = total + held[lax.rem(x + self.nx - m, self.nx) * self.nz + zz].astype(F32)
             summed[zz] = total.astype(summed.dtype)
 
         def step(k):
             add(k)
-            self.along_z(summed, landed, sems, k, False).start()
+            self.along_z(summed, landed, sems, k)
 
         loop(0, self.nz - 1, step)
         add(self.nz - 1)
@@ -359,17 +352,14 @@
     def landed(self, b, held, summed, landed, sems):
         x, z = self.place()
         total = summed[z].astype(F32)
+        arrived(first_blocks(landed, self.nz - 1), sems[3])
         for k in range(self.nz - 1):
-            self.along_z(summed, landed, sems, k, True).wait_recv()
             total = total + landed[lax.rem(z + self.nz - k - 1, self.nz)].astype(F32)
         return total
 
     def sent(self, b, held, summed, landed, sems):
-        def wait(k):
-            loop(1, self.nx, lambda m: self.along_x(b, held, sems, k, m, False).wait_send())
-
-        loop(0, self.nz, wait)
-        loop(0, self.nz - 1, lambda k: self.along_z(summed, landed, sems, k, False).wait_send())
+        left(first_blocks(b, self.nz * (self.nx - 1)), sems[0])
+        left(first_blocks(landed, self.nz - 1), sems[2])
 
 
 class SumAlong:
@@ -377,33 +367,31 @@
         self.n, self.along_z = (NZ if along_z else n // NZ), along_z
 
     def sems(self):
-        return [dma(self.n), dma(self.n)]
+        return [dma(), dma()]
 
     def place(self):
         me = lax.axis_index(SEQ)
         return lax.rem(me, NZ) if self.along_z else me // NZ
 
-    def copy(self, src, held, sems, k, received):
+    def send(self, src, held, sems, k):
         me = lax.axis_index(SEQ)
-        here = self.place()
-        at = lax.rem(here + self.n - k, self.n) if received else here
-        to = lax.rem(here + k, self.n)
+        to = lax.rem(self.place() + k, self.n)
         to = me // NZ * NZ + to if self.along_z else to * NZ + lax.rem(me, NZ)
-        return remote(src, held.at[at], sems[0].at[k], sems[1].at[k], {SEQ: to})
+        remote(src, held.at[self.place()], sems[0], sems[1], {SEQ: to}).start()
 
     def start(self, src, held, sems):
-        loop(1, self.n, lambda k: self.copy(src, held, sems, k, False).start())
+        loop(1, self.n, lambda k: self.send(src, held, sems, k))
         held[self.place()] = src[...]
 
     def landed(self, src, held, sems):
-        loop(1, self.n, lambda k: self.copy(src, held, sems, k, True).wait_recv())
+        arrived(first_blocks(held, self.n - 1), sems[1])
         total = held[0]
         for at in range(1, self.n):
             total = total + held[at]
         return total
 
     def sent(self, src, held, sems):
-        loop(1, self.n, lambda k: self.copy(src, held, sems, k, False).wait_send())
+        left(first_blocks(held, self.n - 1), sems[0])
 
 
 def bound(job, sems, refs):
@@ -453,7 +441,9 @@
     ny, nz, nx = n_var // 2, NZ, n_seq // NZ
 
     at_cut = lambda j: pl.ds(pl.multiple_of(j * cut, cut), cut)
-    weight = lambda w: RingVar(n_var, lambda o, j: o.at[j, :, pl.ds(w * HD, HD)])
+    weight = lambda w: RingVar(
+        n_var, lambda o, j: o.at[j, :, pl.ds(w * HD, HD)], lambda o, n: o.at[pl.ds(0, n), :, pl.ds(w * HD, HD)]
+    )
     jobs = dict(
         tokens=Direct(VAR, n_var, lambda x, j: x.at[:, :, at_cut(j)], slot),
         scores=GatherVar(n_var),
@@ -469,10 +459,10 @@
         d_pooled=GatherVar(n_var),
         dmix=ReduceVar(n_var),
         dscore=GatherVar(n_var),
-        back=Direct(VAR, n_var, slot, lambda o, j: o.at[:, :, at_cut(j)]),
+        back=Direct(VAR, n_var, slot, lambda o, j: o.at[:, :, at_cut(j)], lambda o, n: o.at[:, :, pl.ds(0, n * cut)]),
         query_z=SumAlong(n_seq, True),
         query_x=SumAlong(n_seq, False),
-        query=GatherVar(n_var, lambda o, j: o.at[:, at_cut(j)]),
+        query=GatherVar(n_var, lambda o, j: o.at[:, at_cut(j)], lambda o, n: o.at[:, pl.ds(0, n * cut)]),
     )
 
     block = lambda n, r=line, c=HD, t=BF16: ((n, r, c), t)
@@ -507,8 +497,8 @@
         dp_all=block(n_var),
         d_summary=block(groups, tall, cut),
         dmix0=dmix[0], dmix1=dmix[1], dmix2=dmix[2], dmix3=dmix[3],
-        dscore_own=((8, lanes), F32),
-        dscore_all=block(n_var, 8, lanes, F32),
+        dscore_own=((16, lanes // 2), BF16),
+        dscore_all=block(n_var, 16, lanes // 2),
         back_b=((n_var, per, rows, cut), BF16),
         query_part=((heads, cut), F32),
         query_line=((heads, cut), F32),
@@ -706,21 +696,23 @@
             part = dot(r.mix_tall[g], r.d_summary[g]).astype(BF16)
             r.back_b[:, :, g * 16 : (g + 1) * 16, :] = part.reshape(n_var, per, 16, cut)
         j.dmix.push()
-        j.back.far(4)
+        j.back.some(0, 1, 2)
         dmix = j.dmix.landed()
         mixw = r.mix[i]
         dscore = mixw * (dmix - over_vars(jnp.add, mixw * dmix)) * factor
-        r.dscore_own[...] = dscore.astype(BF16).astype(F32)
+        r.dscore_own[...] = jnp.concatenate([dscore[:, : lanes // 2], dscore[:, lanes // 2 :]], axis=0).astype(BF16)
         j.dscore.start()
-        j.back.near(4)
+        j.back.some(3)
         j.dscore.middle()
         j.dscore.landed()
+        j.back.some(7, 6)
 
         query_part = jnp.zeros((heads, cut), F32)
         mine = jnp.zeros((heads, per * rows), F32)
         lane, column = iota((lanes, per * rows), 0) - i * chunk, iota((lanes, per * rows), 1)
         for g in range(groups):
-            dscore = r.dscore_all[g * octets : (g + 1) * octets].reshape(heads, lanes).astype(BF16)
+            halves = r.dscore_all[g * octets : (g + 1) * octets].astype(F32)
+            dscore = jnp.concatenate([halves[:, :8], halves[:, 8:]], axis=2).reshape(heads, lanes).astype(BF16)
             query_part = query_part + dot(dscore, t_group(g))
             at_lane = column // rows * 16 + lax.rem(column, 16)
             here = (lane == at_lane) & (lax.rem(column, rows) // 16 == g)
@@ -732,6 +724,7 @@
         j.query_x.start()
         r.query_done[...] = j.query_x.landed()
         j.query.start()
+        j.back.some(8, 5, 4)
         j.query.middle()
         for job in (j.tokens, j.pooled, j.normed, *ring, j.kv, j.dkv, j.grad, j.d_pooled, j.dmix, j.dscore):
             job.sent()

time: 223 us -> 210 us (0.942)
  Pallas kernels: 217 us -> 205 us
    pallas_call x1, Pallas kernels: 217 us -> 205 us  [program(): pl.pallas_call(kernel, name='encoder', out_shape=[jax.ShapeDtypeStruct(*r...]
where the time goes in v3:
time: 210 us
  Pallas kernels  205 us (98%)
    pallas_call x1, Pallas kernels, program(): pl.pallas_call(kernel, name='encoder', out_shape=[jax.ShapeDtypeStruct(*r...  205 us

profile of v3, /device:TPU:1, one launch (start us, length us, event | category | flops | bytes accessed | tf_op | source)
XLA Modules:
  0.0 210.0 jit_solution(15537154349360876554)
XLA Ops:
  0.6 204.7 %encoder.1 = (bf16[128,128]{1,0:T(8,128)(2,1)}, bf16[3,64,4096]{2,1,0:T(8,128)(2,1)}, bf16[32,192]{1,0:T(8,128)(2,1)}, f32[32,4096]{1,0:T(8,128)}) custom-call(bf16[3,64,4096]{2,1,0:T(8,128)(2,1)} %tok.1, bf16[32,4096]{1,0:T(8,128)(2,1)} %aq.1, bf16[256,128]{1,0:T(8,128)(2,1)} %av.1, bf16[256,128]{1,0:T(8,128)(2,1)} %wq.1, bf16[256,128]{1,0:T(8,128)(2,1)} %wk.1, ...), custom_call_target="tpu_custom_call" | custom-call | tf_op jit(solution)/shard_map/encoder/pallas_call | solution.py:739
  205.3 0.0 copy-start
  205.3 1.7 fusion
  207.0 0.0 copy-done
  207.0 0.0 copy-start.2
  207.0 0.0 copy-start.1
  207.0 1.5 add_convert_fusion
  208.5 0.0 copy-done.2
  208.5 0.6 copy.13
  209.2 0.0 copy-done.1
  209.2 0.8 copy.14
Async XLA Ops:
  205.3 1.7 copy-start
  207.0 1.5 copy-start.2
  207.0 2.1 %copy-start.1 = (f32[32,4096]{1,0:T(8,128)S(1)}, f32[32,4096]{1,0:T(8,128)}, u32[]{:S(2)}) copy-start(f32[32,4096]{1,0:T(8,128)} %get-tuple-element.16) | copy-start | bytes 1572868

commit v4 on v3

--- a/solution.py
+++ b/solution.py
@@ -15,6 +15,7 @@
 F32 = jnp.float32
 BF16 = jnp.bfloat16
 VAR, SEQ = "var", "seq"
+X, Z = "x", "z"
 NT = ((1,), (1,))
 TN = ((0,), (0,))
 
@@ -37,6 +38,10 @@
     return ref.at[j]
 
 
+def whole(ref, j):
+    return ref
+
+
 def dma(*shape):
     return pltpu.SemaphoreType.DMA(shape)
 
@@ -60,17 +65,27 @@
     def sems(self):
         return [dma(), dma(), dma()]
 
+    def here(self):
+        if self.axis == VAR:
+            return lax.axis_index(VAR)
+        return lax.axis_index(SEQ) // NZ if self.axis == X else lax.rem(lax.axis_index(SEQ), NZ)
+
+    def device(self, to):
+        if self.axis == VAR:
+            return {VAR: to}
+        me = lax.axis_index(SEQ)
+        return {SEQ: to * NZ + lax.rem(me, NZ) if self.axis == X else me // NZ * NZ + to}
+
     def peers(self):
-        me = lax.axis_index(self.axis)
-        return [(self.n - 1, lambda k: {self.axis: lax.rem(me + k + 1, self.n)})]
+        return [(self.n - 1, lambda k: self.device(lax.rem(self.here() + k + 1, self.n)))]
 
     def send(self, x, o, sems, k):
-        me = lax.axis_index(self.axis)
+        me = self.here()
         to = lax.rem(me + k, self.n)
-        remote(self.src(x, to), self.dst(o, me), sems[0], sems[1], {self.axis: to}).start()
+        remote(self.src(x, to), self.dst(o, me), sems[0], sems[1], self.device(to)).start()
 
     def own(self, x, o, sems):
-        me = lax.axis_index(self.axis)
+        me = self.here()
         return pltpu.make_async_copy(self.src(x, me), self.dst(o, me), sems[2])
 
     def start(self, x, o, sems):
@@ -360,38 +375,6 @@
     def sent(self, b, held, summed, landed, sems):
         left(first_blocks(b, self.nz * (self.nx - 1)), sems[0])
         left(first_blocks(landed, self.nz - 1), sems[2])
-
-
-class SumAlong:
-    def __init__(self, n, along_z):
-        self.n, self.along_z = (NZ if along_z else n // NZ), along_z
-
-    def sems(self):
-        return [dma(), dma()]
-
-    def place(self):
-        me = lax.axis_index(SEQ)
-        return lax.rem(me, NZ) if self.along_z else me // NZ
-
-    def send(self, src, held, sems, k):
-        me = lax.axis_index(SEQ)
-        to = lax.rem(self.place() + k, self.n)
-        to = me // NZ * NZ + to if self.along_z else to * NZ + lax.rem(me, NZ)
-        remote(src, held.at[self.place()], sems[0], sems[1], {SEQ: to}).start()
-
-    def start(self, src, held, sems):
-        loop(1, self.n, lambda k: self.send(src, held, sems, k))
-        held[self.place()] = src[...]
-
-    def landed(self, src, held, sems):
-        arrived(first_blocks(held, self.n - 1), sems[1])
-        total = held[0]
-        for at in range(1, self.n):
-            total = total + held[at]
-        return total
-
-    def sent(self, src, held, sems):
-        left(first_blocks(held, self.n - 1), sems[0])
 
 
 def bound(job, sems, refs):
@@ -439,8 +422,10 @@
     row_count = n_seq * own
     at_once = 16 // own
     ny, nz, nx = n_var // 2, NZ, n_seq // NZ
+    share = heads // nx
 
     at_cut = lambda j: pl.ds(pl.multiple_of(j * cut, cut), cut)
+    few = lambda j: pl.ds(pl.multiple_of(j * share, share), share)
     weight = lambda w: RingVar(
         n_var, lambda o, j: o.at[j, :, pl.ds(w * HD, HD)], lambda o, n: o.at[pl.ds(0, n), :, pl.ds(w * HD, HD)]
     )
@@ -459,10 +444,11 @@
         d_pooled=GatherVar(n_var),
         dmix=ReduceVar(n_var),
         dscore=GatherVar(n_var),
-        back=Direct(VAR, n_var, slot, lambda o, j: o.at[:, :, at_cut(j)], lambda o, n: o.at[:, :, pl.ds(0, n * cut)]),
-        query_z=SumAlong(n_seq, True),
-        query_x=SumAlong(n_seq, False),
+        back=Direct(VAR, n_var, slot, lambda o, j: o.at[:, at_cut(j)], lambda o, n: o.at[:, pl.ds(0, n * cut)]),
+        query_z=Direct(Z, nz, whole),
+        query_x=Direct(X, nx, lambda x, j: x.at[few(j)]),
         query=GatherVar(n_var, lambda o, j: o.at[:, at_cut(j)], lambda o, n: o.at[:, pl.ds(0, n * cut)]),
+        query_all=Direct(X, nx, whole, lambda o, j: o.at[few(j)], lambda o, n: o.at[pl.ds(0, n * share)]),
     )
 
     block = lambda n, r=line, c=HD, t=BF16: ((n, r, c), t)
@@ -474,8 +460,8 @@
     dmix = through(n_var, 8, lanes, F32)
     buffers = dict(
         grouped=((n_var, per, rows, cut), BF16),
-        s_own=((heads, 256), F32),
-        s_all=block(n_var, heads, 256, F32),
+        s_own=((heads, (per + 1) * rows), BF16),
+        s_all=block(n_var, heads, (per + 1) * rows),
         value_all=block(n_seq, cut, HD),
         mix=block(n_var, 8, lanes, F32),
         mix_wide=block(groups, tall, lanes),
@@ -499,16 +485,17 @@
         dmix0=dmix[0], dmix1=dmix[1], dmix2=dmix[2], dmix3=dmix[3],
         dscore_own=((16, lanes // 2), BF16),
         dscore_all=block(n_var, 16, lanes // 2),
-        back_b=((n_var, per, rows, cut), BF16),
+        back_b=block(n_var, per * rows, cut),
         query_part=((heads, cut), F32),
         query_line=((heads, cut), F32),
-        query_done=((heads, cut), F32),
+        query_done=((share, cut), F32),
+        query_wide=((share, width), F32),
         query_z=block(nz, heads, cut, F32),
-        query_x=block(nx, heads, cut, F32),
+        query_x=block(nx, share, cut, F32),
     )
     results = dict(
         attended=((row_count, HD), BF16),
-        mixed=(tokens.shape, BF16),
+        mixed=((per * rows, width), BF16),
         dscore=((heads, per * rows), BF16),
         d_query=((heads, width), F32),
     )
@@ -535,7 +522,8 @@
             back=(r.back_b, r.mixed),
             query_z=(r.query_part, r.query_z),
             query_x=(r.query_line, r.query_x),
-            query=(r.query_done, r.d_query),
+            query=(r.query_done, r.query_wide),
+            query_all=(r.query_wide, r.d_query),
         )
         left, ready_jobs = list(rest[len(names) :]), {}
         for (name, job), wanted in zip(jobs.items(), job_sems):
@@ -550,9 +538,10 @@
         i = lax.axis_index(VAR)
         greeted = barrier(jobs["tokens"].peers() + jobs["value"].peers())
 
-        rows_here = [tok[v, g * 16 : (g + 1) * 16, :] for g in range(groups) for v in range(per)]
-        local = dot(aq[...], jnp.concatenate(rows_here, axis=0), NT) * factor
-        r.s_own[...] = jnp.concatenate([local, jnp.zeros((heads, 256 - per * rows), F32)], axis=1)
+        local = dot(aq[...], tok[...].reshape(per * rows, width), NT) * factor
+        scaled = [local[:, v * rows : (v + 1) * rows] for v in range(per)]
+        top = functools.reduce(jnp.maximum, scaled).astype(BF16).astype(F32)
+        r.s_own[...] = jnp.concatenate([*[jnp.exp(part - top) for part in scaled], top], axis=1).astype(BF16)
         greeted()
         j.scores.start()
         j.value.start()
@@ -570,9 +559,12 @@
         to_heads = ones(to == lax.rem(at, 16) * heads + at // 16)
 
         j.scores.landed()
+        scores = r.s_all[...].astype(F32)
         for g in range(groups):
-            z = jnp.concatenate([r.s_all[n, :, g * chunk : (g + 1) * chunk] for n in range(n_var)], axis=1)
-            e = jnp.exp(z - over_vars(jnp.maximum, z))
+            picked = lambda n, v: scores[n, :, v * rows + g * 16 : v * rows + (g + 1) * 16]
+            over = lambda pick: jnp.concatenate([pick(n, v) for n in range(n_var) for v in range(per)], axis=1)
+            tops = over(lambda n, v: picked(n, per))
+            e = over(picked) * jnp.exp(tops - over_vars(jnp.maximum, tops))
             mixw = e / over_vars(jnp.add, e)
             for o in range(octets):
                 r.mix[g * octets + o] = mixw[o * 8 : (o + 1) * 8]
@@ -687,22 +679,24 @@
             for g in range(groups):
                 r.d_summary[g, here, :] = part[g * 16 : (g + 1) * 16]
         for g in range(groups):
+            part = dot(r.mix_tall[g], r.d_summary[g]).astype(BF16).reshape(n_var, per, 16, cut)
+            for v in range(per):
+                r.back_b[:, v * rows + g * 16 : v * rows + (g + 1) * 16, :] = part[:, v]
+        j.back.some(0, 1, 2)
+        for g in range(groups):
             cross = dot(r.d_summary[g], t_group(g), NT).reshape(heads, 16, lanes)
             dmix = jnp.sum(jnp.where(wide_mask[None], cross, 0.0), axis=1)
             for o in range(octets):
                 r.dmix0[g * octets + o] = dmix[o * 8 : (o + 1) * 8]
         j.dmix.start()
-        for g in range(groups):
-            part = dot(r.mix_tall[g], r.d_summary[g]).astype(BF16)
-            r.back_b[:, :, g * 16 : (g + 1) * 16, :] = part.reshape(n_var, per, 16, cut)
         j.dmix.push()
-        j.back.some(0, 1, 2)
+        j.back.some(3)
         dmix = j.dmix.landed()
         mixw = r.mix[i]
         dscore = mixw * (dmix - over_vars(jnp.add, mixw * dmix)) * factor
         r.dscore_own[...] = jnp.concatenate([dscore[:, : lanes // 2], dscore[:, lanes // 2 :]], axis=0).astype(BF16)
         j.dscore.start()
-        j.back.some(3)
+        j.back.some(4)
         j.dscore.middle()
         j.dscore.landed()
         j.back.some(7, 6)
@@ -720,18 +714,23 @@
         r.query_part[...] = query_part
         j.query_z.start()
         r.dscore[...] = mine.astype(BF16)
-        r.query_line[...] = j.query_z.landed()
+        j.query_z.landed()
+        r.query_line[...] = jnp.sum(r.query_z[...], axis=0)
         j.query_x.start()
-        r.query_done[...] = j.query_x.landed()
+        j.query_x.landed()
+        r.query_done[...] = jnp.sum(r.query_x[...], axis=0)
         j.query.start()
-        j.back.some(8, 5, 4)
+        j.back.some(8, 5)
         j.query.middle()
         for job in (j.tokens, j.pooled, j.normed, *ring, j.kv, j.dkv, j.grad, j.d_pooled, j.dmix, j.dscore):
             job.sent()
+        j.query.landed()
+        j.query_all.start()
         j.query_z.sent()
         j.query_x.sent()
-        j.query.landed()
         j.query.sent()
+        j.query_all.landed()
+        j.query_all.sent()
         j.back.landed()
         j.back.sent()
 
@@ -756,8 +755,7 @@
         n_var, n_seq, tokens, agg_query, agg_value, w_query, w_key, w_value,
         gain.reshape(heads, HD), d_out.reshape(-1, HD),
     )
-    through_scores = dot(dscore, agg_query, TN).reshape(tokens.shape)
-    d_tokens = (mixed.astype(F32) + through_scores).astype(BF16)
+    d_tokens = (mixed.astype(F32) + dot(dscore, agg_query, TN)).astype(BF16).reshape(tokens.shape)
     return (attended.reshape(d_out.shape), d_tokens, d_query)
 
 

time: 210 us -> 205 us (0.976)
  Pallas kernels: 205 us -> 199 us
    pallas_call x1, Pallas kernels: 205 us -> 199 us  [program(): pl.pallas_call(kernel, name='encoder', out_shape=[jax.ShapeDtypeStruct(*r...]
where the time goes in v4:
time: 205 us
  Pallas kernels  199 us (97%)
  matrix products  3.22 us (2%)
    pallas_call x1, Pallas kernels, program(): pl.pallas_call(kernel, name='encoder', out_shape=[jax.ShapeDtypeStruct(*r...  199 us

profile of v4, /device:TPU:1, one launch (start us, length us, event | category | flops | bytes accessed | tf_op | source)
XLA Modules:
  0.0 204.6 jit_solution(6175039462843782539)
XLA Ops:
  0.6 0.0 copy-start
  0.6 199.3 %encoder.1 = (bf16[128,128]{1,0:T(8,128)(2,1)}, bf16[192,4096]{1,0:T(8,128)(2,1)}, bf16[32,192]{1,0:T(8,128)(2,1)}, f32[32,4096]{1,0:T(8,128)}) custom-call(bf16[3,64,4096]{2,1,0:T(8,128)(2,1)} %tok.1, bf16[32,4096]{1,0:T(8,128)(2,1)} %aq.1, bf16[256,128]{1,0:T(8,128)(2,1)} %av.1, bf16[256,128]{1,0:T(8,128)(2,1)} %wq.1, bf16[256,128]{1,0:T(8,128)(2,1)} %wk.1, ...), custom_call_target="tpu_custom_call" | custom-call | tf_op jit(solution)/shard_map/encoder/pallas_call | solution.py:738
  200.0 0.0 copy-done
  200.0 0.0 copy-start.2
  200.0 0.0 copy-start.1
  200.0 3.2 %fusion = bf16[192,4096]{1,0:T(8,128)(2,1)} fusion(bf16[32,192]{1,0:T(8,128)(2,1)} %get-tuple-element.9, bf16[32,4096]{1,0:T(8,128)(2,1)S(1)} %copy-done, bf16[192,4096]{1,0:T(8,128)(2,1)} %get-tuple-element.8), kind=kOutput, calls=%fused_computation.1 | convolution fusion | flops 52690944 | bytes 3420160 | tf_op jit(solution)/shard_map/dot_general | solution.py:398
  203.2 0.0 copy-done.2
  203.2 0.6 copy.13
  203.8 0.0 copy-done.1
  203.8 0.8 copy.14
Async XLA Ops:
  0.6 199.3 %copy-start = (bf16[32,4096]{1,0:T(8,128)(2,1)S(1)}, bf16[32,4096]{1,0:T(8,128)(2,1)}, u32[]{:S(2)}) copy-start(bf16[32,4096]{1,0:T(8,128)(2,1)} %aq.1) | copy-start | bytes 786436
  200.0 3.2 %copy-start.2 = (bf16[128,128]{1,0:T(8,128)(2,1)S(1)}, bf16[128,128]{1,0:T(8,128)(2,1)}, u32[]{:S(2)}) copy-start(bf16[128,128]{1,0:T(8,128)(2,1)} %get-tuple-element.7) | copy-start | bytes 98308
  200.0 3.8 %copy-start.1 = (f32[32,4096]{1,0:T(8,128)S(1)}, f32[32,4096]{1,0:T(8,128)}, u32[]{:S(2)}) copy-start(f32[32,4096]{1,0:T(8,128)} %get-tuple-element.16) | copy-start | bytes 1572868

commit v5 on v4

--- a/solution.py
+++ b/solution.py
@@ -546,6 +546,8 @@
         j.scores.start()
         j.value.start()
         j.tokens.start()
+        for w in ring:
+            w.start()
         j.scores.middle()
         j.value.middle()
 
@@ -577,8 +579,6 @@
         j.scores.sent()
         j.value.sent()
         j.tokens.landed()
-        for w in ring:
-            w.start()
 
         for g in range(groups):
             r.summary[g] = dot(r.mix_wide[g], t_group(g)).astype(BF16)

time: 205 us -> 203 us (level)
    pallas_call x1, Pallas kernels: 199 us -> 197 us  [program(): pl.pallas_call(kernel, name='encoder', out_shape=[jax.ShapeDtypeStruct(*r...]
where the time goes in v5:
time: 203 us; the launch traced here: 202 us
  Pallas kernels  197 us (97%)
  matrix products  3.22 us (2%)
    pallas_call x1, Pallas kernels, program(): pl.pallas_call(kernel, name='encoder', out_shape=[jax.ShapeDtypeStruct(*r...  197 us

profile of v5, /device:TPU:1, one launch (start us, length us, event | category | flops | bytes accessed | tf_op | source)
XLA Modules:
  0.0 201.9 jit_solution(11704793245038758884)
XLA Ops:
  0.6 0.0 copy-start
  0.6 196.5 %encoder.1 = (bf16[128,128]{1,0:T(8,128)(2,1)}, bf16[192,4096]{1,0:T(8,128)(2,1)}, bf16[32,192]{1,0:T(8,128)(2,1)}, f32[32,4096]{1,0:T(8,128)}) custom-call(bf16[3,64,4096]{2,1,0:T(8,128)(2,1)} %tok.1, bf16[32,4096]{1,0:T(8,128)(2,1)} %aq.1, bf16[256,128]{1,0:T(8,128)(2,1)} %av.1, bf16[256,128]{1,0:T(8,128)(2,1)} %wq.1, bf16[256,128]{1,0:T(8,128)(2,1)} %wk.1, ...), custom_call_target="tpu_custom_call" | custom-call | tf_op jit(solution)/shard_map/encoder/pallas_call | solution.py:738
  197.2 0.0 copy-done
  197.2 0.0 copy-start.2
  197.2 0.0 copy-start.1
  197.2 3.2 %fusion = bf16[192,4096]{1,0:T(8,128)(2,1)} fusion(bf16[32,192]{1,0:T(8,128)(2,1)} %get-tuple-element.9, bf16[32,4096]{1,0:T(8,128)(2,1)S(1)} %copy-done, bf16[192,4096]{1,0:T(8,128)(2,1)} %get-tuple-element.8), kind=kOutput, calls=%fused_computation.1 | convolution fusion | flops 52690944 | bytes 3420160 | tf_op jit(solution)/shard_map/dot_general | solution.py:398
  200.4 0.0 copy-done.2
  200.4 0.6 copy.13
  201.1 0.0 copy-done.1
  201.1 0.8 copy.14
Async XLA Ops:
  0.6 196.6 %copy-start = (bf16[32,4096]{1,0:T(8,128)(2,1)S(1)}, bf16[32,4096]{1,0:T(8,128)(2,1)}, u32[]{:S(2)}) copy-start(bf16[32,4096]{1,0:T(8,128)(2,1)} %aq.1) | copy-start | bytes 786436
  197.2 3.2 %copy-start.2 = (bf16[128,128]{1,0:T(8,128)(2,1)S(1)}, bf16[128,128]{1,0:T(8,128)(2,1)}, u32[]{:S(2)}) copy-start(bf16[128,128]{1,0:T(8,128)(2,1)} %get-tuple-element.7) | copy-start | bytes 98308
  197.2 3.9 %copy-start.1 = (f32[32,4096]{1,0:T(8,128)S(1)}, f32[32,4096]{1,0:T(8,128)}, u32[]{:S(2)}) copy-start(f32[32,4096]{1,0:T(8,128)} %get-tuple-element.16) | copy-start | bytes 1572868

commit v6 on v5

--- a/solution.py
+++ b/solution.py
@@ -496,7 +496,7 @@
     results = dict(
         attended=((row_count, HD), BF16),
         mixed=((per * rows, width), BF16),
-        dscore=((heads, per * rows), BF16),
+        through_scores=((per * rows, width), BF16),
         d_query=((heads, width), F32),
     )
     names = [*results, *buffers]
@@ -713,7 +713,6 @@
             mine = mine + dot(dscore, ones(here))
         r.query_part[...] = query_part
         j.query_z.start()
-        r.dscore[...] = mine.astype(BF16)
         j.query_z.landed()
         r.query_line[...] = jnp.sum(r.query_z[...], axis=0)
         j.query_x.start()
@@ -726,6 +725,7 @@
             job.sent()
         j.query.landed()
         j.query_all.start()
+        r.through_scores[...] = dot(mine.astype(BF16), aq[...], TN).astype(BF16)
         j.query_z.sent()
         j.query_x.sent()
         j.query.sent()
@@ -751,11 +751,11 @@
 
 def per_device(n_var, n_seq, tokens, agg_query, agg_value, w_query, w_key, w_value, gain, d_out):
     heads = agg_query.shape[0]
-    attended, mixed, dscore, d_query = program(
+    attended, mixed, through_scores, d_query = program(
         n_var, n_seq, tokens, agg_query, agg_value, w_query, w_key, w_value,
         gain.reshape(heads, HD), d_out.reshape(-1, HD),
     )
-    d_tokens = (mixed.astype(F32) + dot(dscore, agg_query, TN)).astype(BF16).reshape(tokens.shape)
+    d_tokens = (mixed.astype(F32) + through_scores.astype(F32)).astype(BF16).reshape(tokens.shape)
     return (attended.reshape(d_out.shape), d_tokens, d_query)
 
 

time: 203 us -> 205 us (level)
  other arithmetic: 0 us -> 3.62 us
  matrix products: 3.22 us -> 0 us
    convert_element_type x0 -> x1, other arithmetic: none -> 3.62 us  [per_device(): (mixed.astype(F32) + through_scores.astype(F32)).astype(BF16)]
    dot_general x1 -> x0, matrix products: 3.22 us -> none  [dot(): return lax.dot_general(a, b, (dims, ((), ())), preferred_element_type=F32)]
where the time goes in v6:
time: 205 us; the launch traced here: 204 us
  Pallas kernels  198 us (97%)
  other arithmetic  3.62 us (2%)
    pallas_call x1, Pallas kernels, program(): pl.pallas_call(kernel, name='encoder', out_shape=[jax.ShapeDtypeStruct(*r...  198 us

profile of v6, /device:TPU:1, one launch (start us, length us, event | category | flops | bytes accessed | tf_op | source)
XLA Modules:
  0.0 203.5 jit_solution(15274292040399196140)
XLA Ops:
  0.6 197.8 %encoder.1 = (bf16[128,128]{1,0:T(8,128)(2,1)}, bf16[192,4096]{1,0:T(8,128)(2,1)}, bf16[192,4096]{1,0:T(8,128)(2,1)}, f32[32,4096]{1,0:T(8,128)}) custom-call(bf16[3,64,4096]{2,1,0:T(8,128)(2,1)} %tok.1, bf16[32,4096]{1,0:T(8,128)(2,1)} %aq.1, bf16[256,128]{1,0:T(8,128)(2,1)} %av.1, bf16[256,128]{1,0:T(8,128)(2,1)} %wq.1, bf16[256,128]{1,0:T(8,128)(2,1)} %wk.1, ...), custom_call_target="tpu_custom_call" | custom-call | tf_op jit(solution)/shard_map/encoder/pallas_call | solution.py:738
  198.5 0.0 copy-start.1
  198.5 0.0 copy-start
  198.5 3.6 %add_convert_fusion = bf16[192,4096]{1,0:T(8,128)(2,1)} fusion(bf16[192,4096]{1,0:T(8,128)(2,1)} %get-tuple-element.9, bf16[192,4096]{1,0:T(8,128)(2,1)} %get-tuple-element.8), kind=kLoop, calls=%fused_computation | loop fusion | flops 3145728 | bytes 4718592 | tf_op jit(solution)/shard_map/convert_element_type | solution.py:758
  202.1 0.0 copy-done.1
  202.1 0.6 copy.13
  202.7 0.0 copy-done
  202.8 0.8 copy.14
Async XLA Ops:
  198.5 3.6 %copy-start.1 = (bf16[128,128]{1,0:T(8,128)(2,1)S(1)}, bf16[128,128]{1,0:T(8,128)(2,1)}, u32[]{:S(2)}) copy-start(bf16[128,128]{1,0:T(8,128)(2,1)} %get-tuple-element.7) | copy-start | bytes 98308
  198.5 4.3 %copy-start = (f32[32,4096]{1,0:T(8,128)S(1)}, f32[32,4096]{1,0:T(8,128)}, u32[]{:S(2)}) copy-start(f32[32,4096]{1,0:T(8,128)} %get-tuple-element.16) | copy-start | bytes 1572868
